TPU v7x, 256 devices: a whole 4x4x8 slice. The times are simulated.
256 devices in a mesh: ctx: 32 (over x, z), tp: 8 (over y, core).
Axes of the slice: x: 4, y: 4, z: 8, core: 2. Of those that a mesh axis runs over, the one named last changes fastest.
Arguments:
- hidden_in: bfloat16 [16384, 4096], P('ctx', 'tp'), may hold values from -6 to 6
- w_qkv: bfloat16 [3, 4096, 2048], P(None, None, 'tp'), may hold values from -0.09375 to 0.09375
- lr_weight: bfloat16 [4096, 16], P(None, 'tp'), may hold values from -0.09375 to 0.09375
- inner_lr: float32 [16], P('tp'), may hold values from 0.0005 to 0.5
- init_state: float32 [16, 128, 128], P('tp'), may hold values from -0.5 to 0.5
- norm_gain: float32 [16, 128], P('tp'), may hold values from 0.1 to 1.9
- w_out: bfloat16 [2048, 4096], P('tp'), may hold values from -0.125 to 0.125
Outputs:
- mixed: bfloat16 [16384, 4096], P('ctx', 'tp')
All inputs are finite; a program needn't handle non-finite values.
Results may differ from a plain program's by a relative error of at most 0.019.
Values may be sent and summed in bfloat16 or wider, within the bound.
A program may use at most 64 MiB of HBM per device.

v0:
```python
import jax
import jax.numpy as jnp
from jax import lax
from jax.sharding import PartitionSpec as P

MB = 16


def from_behind(block, axis, distance):
    devices = range(lax.axis_size(axis))
    route = [(i - distance, i) for i in devices if i - distance in devices]
    return lax.ppermute(block, axis, route)


def normalize(v):
    return v / jnp.sqrt(v.shape[-1] * (jnp.mean(v * v, -1, keepdims=True) + 1e-06))


def mm(form, a, b):
    return jnp.einsum(form, a, b, precision=lax.Precision.HIGHEST)


def descend(state, keys, targets, rates):
    err = mm("hsi,hij->hsj", keys, state) - targets
    return state - mm("hsi,hsj->hij", keys, rates[:, :, None] * err)


def local(hidden_in, w_qkv, lr_weight, inner_lr, init_state, norm_gain, w_out):
    tok_rows = hidden_in.shape[0]
    head_count = inner_lr.shape[0]
    head_dim = init_state.shape[1]
    local_cols = head_count * head_dim
    block_len = MB
    nblk = tok_rows // block_len
    piece = lax.all_gather(hidden_in, "tp", axis=1, tiled=True)
    proj = jnp.einsum("td,cdj->ctj", piece, w_qkv, preferred_element_type=jnp.float32)
    logit = jnp.dot(piece, lr_weight, preferred_element_type=jnp.float32)
    rate = inner_lr[:, None] * jax.nn.sigmoid(logit).T

    def blocks(m):
        return m.reshape(nblk, block_len, head_count, head_dim).transpose(0, 2, 1, 3)

    queries = blocks(normalize(proj[0].reshape(tok_rows, head_count, head_dim)))
    keys = blocks(normalize(proj[1].reshape(tok_rows, head_count, head_dim)))
    values = blocks(proj[2])
    rate_blocks = rate.reshape(head_count, nblk, block_len).transpose(1, 0, 2)
    identity_map = jnp.broadcast_to(
        jnp.eye(head_dim, dtype=jnp.float32), (head_count, head_dim, head_dim)
    )
    zero_map = jnp.zeros((head_count, head_dim, head_dim), jnp.float32)

    def gather_map_step(carry, block):
        kb, vb, rb = block
        linear = descend(carry[0], kb, jnp.zeros_like(vb), rb)
        offset = descend(carry[1], kb, vb, rb)
        return ((linear, offset), None)

    (linear_map, offset_map), unused = lax.scan(
        gather_map_step, (identity_map, zero_map), (keys, values, rate_blocks)
    )
    position = lax.axis_index("ctx")
    ctx_size = lax.axis_size("ctx")

    def hop(step, incoming):
        outgoing = mm("hij,hjk->hik", linear_map, incoming) + offset_map
        received = from_behind(outgoing, "ctx", 1)
        return jnp.where(position == 0, init_state, received)

    incoming = lax.fori_loop(0, ctx_size - 1, hop, init_state)
    lower = jnp.tril(jnp.ones((block_len, block_len), jnp.float32))

    def output_step(state, block):
        qb, kb, vb, rb = block
        err = mm("hsi,hij->hsj", kb, state) - vb
        scores = mm("hti,hsi->hts", qb, kb) * lower * rb[:, None, :]
        outz = mm("hti,hij->htj", qb, state) - mm("hts,hsj->htj", scores, err)
        state = state - mm("hsi,hsj->hij", kb, rb[:, :, None] * err)
        return (state, outz)

    final, zvals = lax.scan(output_step, incoming, (queries, keys, values, rate_blocks))
    zvals = zvals.transpose(0, 2, 1, 3).reshape(tok_rows, head_count, head_dim)
    normed = zvals / jnp.sqrt(jnp.mean(zvals * zvals, -1, keepdims=True) + 1e-06) * norm_gain
    normed = normed.reshape(tok_rows, local_cols).astype(jnp.bfloat16)
    terms = jnp.dot(normed, w_out, preferred_element_type=jnp.float32)
    mixed = lax.psum_scatter(terms.astype(jnp.bfloat16), "tp", scatter_dimension=1, tiled=True)
    return mixed


def solution(mesh):
    in_specs = (
        P("ctx", "tp"),
        P(None, None, "tp"),
        P(None, "tp"),
        P("tp"),
        P("tp", None, None),
        P("tp", None),
        P("tp", None),
    )
    out_specs = P("ctx", "tp")
    return jax.shard_map(local, mesh=mesh, in_specs=in_specs, out_specs=out_specs, check_vma=False)
```

profile of v0, /device:TPU:2, one launch (start us, length us, event | category | flops | bytes accessed | tf_op | source)
XLA Modules:
  0.0 585.6 jit_solution(8234513274768729853)
XLA Ops:
  8.3 38.6 %all-gather.2.cloned.1.call-done = bf16[512,4096]{1,0:T(8,128)(2,1)} async-done(((bf16[512,512]{1,0:T(8,128)(2,1)}), bf16[512,4096]{1,0:T(8,128)(2,1)}) %all-gather.2.cloned.1.call-update) | async-done | bytes 4194320 | tf_op jit(solution)/shard_map/all_gather | solution.py:35
  72.5 64.8 %while.40 = (s32[]{:T(128)}, f32[2,128,128]{2,1,0:T(8,128)S(1)}, f32[2,128,128]{2,1,0:T(8,128)S(1)}, f32[32,2,16,128]{3,2,1,0:T(8,128)S(1)}, f32[32,2,16]{2,1,0:...) while((s32[]{:T(128)}, f32[2,128,128]{2,1,0:T(8,128)S(1)}, ...), condition=%wide.region_2.3_spmd.clone, body=%wide.region_1.0_spmd.clone.sunk | while | flops 25309188 | bytes 937847 | solution.py:58
  139.7 293.7 %while.38 = (s32[]{:T(128)}, f32[2,128,128]{2,1,0:T(8,128)S(1)}, pred[]{:T(512)}, f32[2,128,128]{2,1,0:T(8,128)S(1)}, f32[2,128,128]{2,1,0:T(8,128)S(1)}, /*index=5*/f32[2,128,128]{2,1,0:T(8,128)S(1)}, s32[]{:T(128)}) while((s32[]{:T(128)}, f32[2,128,128]{2,1,0:T(8,128)S(1)}, pred[]{:T(512)}, f32[2,128,128]{2,1,0:T(8,128)S(1)}, ...), condition=%wide.region_4.5_spmd, body=%wide.region_3.4_spmd.sunk | while | flops 50397184 | bytes 1441910 | solution.py:69
  151.9 7.0 %collective-permute-done = f32[2,128,128]{2,1,0:T(8,128)S(1)} collective-permute-done((f32[2,128,128]{2,1,0:T(8,128)S(1)}, f32[2,128,128]{2,1,0:T(8,128)S(1)}, u32[]{:S(2)}, u32[]{:S(2)}) %collective-permute-start) | collective-permute-done | bytes 131104 | tf_op jit(solution)/shard_map/while/body/eval_jaxpr/ppermute | solution.py:12
  161.1 7.0 %collective-permute-done = f32[2,128,128]{2,1,0:T(8,128)S(1)} collective-permute-done((f32[2,128,128]{2,1,0:T(8,128)S(1)}, f32[2,128,128]{2,1,0:T(8,128)S(1)}, u32[]{:S(2)}, u32[]{:S(2)}) %collective-permute-start) | collective-permute-done | bytes 131104 | tf_op jit(solution)/shard_map/while/body/eval_jaxpr/ppermute | solution.py:12
  170.4 7.0 %collective-permute-done = f32[2,128,128]{2,1,0:T(8,128)S(1)} collective-permute-done((f32[2,128,128]{2,1,0:T(8,128)S(1)}, f32[2,128,128]{2,1,0:T(8,128)S(1)}, u32[]{:S(2)}, u32[]{:S(2)}) %collective-permute-start) | collective-permute-done | bytes 131104 | tf_op jit(solution)/shard_map/while/body/eval_jaxpr/ppermute | solution.py:12
  179.7 7.0 %collective-permute-done = f32[2,128,128]{2,1,0:T(8,128)S(1)} collective-permute-done((f32[2,128,128]{2,1,0:T(8,128)S(1)}, f32[2,128,128]{2,1,0:T(8,128)S(1)}, u32[]{:S(2)}, u32[]{:S(2)}) %collective-permute-start) | collective-permute-done | bytes 131104 | tf_op jit(solution)/shard_map/while/body/eval_jaxpr/ppermute | solution.py:12
  189.0 7.0 %collective-permute-done = f32[2,128,128]{2,1,0:T(8,128)S(1)} collective-permute-done((f32[2,128,128]{2,1,0:T(8,128)S(1)}, f32[2,128,128]{2,1,0:T(8,128)S(1)}, u32[]{:S(2)}, u32[]{:S(2)}) %collective-permute-start) | collective-permute-done | bytes 131104 | tf_op jit(solution)/shard_map/while/body/eval_jaxpr/ppermute | solution.py:12
  198.3 7.6 %collective-permute-done = f32[2,128,128]{2,1,0:T(8,128)S(1)} collective-permute-done((f32[2,128,128]{2,1,0:T(8,128)S(1)}, f32[2,128,128]{2,1,0:T(8,128)S(1)}, u32[]{:S(2)}, u32[]{:S(2)}) %collective-permute-start) | collective-permute-done | bytes 131104 | tf_op jit(solution)/shard_map/while/body/eval_jaxpr/ppermute | solution.py:12
  208.1 8.1 %collective-permute-done = f32[2,128,128]{2,1,0:T(8,128)S(1)} collective-permute-done((f32[2,128,128]{2,1,0:T(8,128)S(1)}, f32[2,128,128]{2,1,0:T(8,128)S(1)}, u32[]{:S(2)}, u32[]{:S(2)}) %collective-permute-start) | collective-permute-done | bytes 131104 | tf_op jit(solution)/shard_map/while/body/eval_jaxpr/ppermute | solution.py:12
  218.5 7.3 %collective-permute-done = f32[2,128,128]{2,1,0:T(8,128)S(1)} collective-permute-done((f32[2,128,128]{2,1,0:T(8,128)S(1)}, f32[2,128,128]{2,1,0:T(8,128)S(1)}, u32[]{:S(2)}, u32[]{:S(2)}) %collective-permute-start) | collective-permute-done | bytes 131104 | tf_op jit(solution)/shard_map/while/body/eval_jaxpr/ppermute | solution.py:12
  228.0 7.0 %collective-permute-done = f32[2,128,128]{2,1,0:T(8,128)S(1)} collective-permute-done((f32[2,128,128]{2,1,0:T(8,128)S(1)}, f32[2,128,128]{2,1,0:T(8,128)S(1)}, u32[]{:S(2)}, u32[]{:S(2)}) %collective-permute-start) | collective-permute-done | bytes 131104 | tf_op jit(solution)/shard_map/while/body/eval_jaxpr/ppermute | solution.py:12
  237.3 7.0 %collective-permute-done = f32[2,128,128]{2,1,0:T(8,128)S(1)} collective-permute-done((f32[2,128,128]{2,1,0:T(8,128)S(1)}, f32[2,128,128]{2,1,0:T(8,128)S(1)}, u32[]{:S(2)}, u32[]{:S(2)}) %collective-permute-start) | collective-permute-done | bytes 131104 | tf_op jit(solution)/shard_map/while/body/eval_jaxpr/ppermute | solution.py:12
  246.6 7.0 %collective-permute-done = f32[2,128,128]{2,1,0:T(8,128)S(1)} collective-permute-done((f32[2,128,128]{2,1,0:T(8,128)S(1)}, f32[2,128,128]{2,1,0:T(8,128)S(1)}, u32[]{:S(2)}, u32[]{:S(2)}) %collective-permute-start) | collective-permute-done | bytes 131104 | tf_op jit(solution)/shard_map/while/body/eval_jaxpr/ppermute | solution.py:12
  255.8 7.0 %collective-permute-done = f32[2,128,128]{2,1,0:T(8,128)S(1)} collective-permute-done((f32[2,128,128]{2,1,0:T(8,128)S(1)}, f32[2,128,128]{2,1,0:T(8,128)S(1)}, u32[]{:S(2)}, u32[]{:S(2)}) %collective-permute-start) | collective-permute-done | bytes 131104 | tf_op jit(solution)/shard_map/while/body/eval_jaxpr/ppermute | solution.py:12
  265.1 7.0 %collective-permute-done = f32[2,128,128]{2,1,0:T(8,128)S(1)} collective-permute-done((f32[2,128,128]{2,1,0:T(8,128)S(1)}, f32[2,128,128]{2,1,0:T(8,128)S(1)}, u32[]{:S(2)}, u32[]{:S(2)}) %collective-permute-start) | collective-permute-done | bytes 131104 | tf_op jit(solution)/shard_map/while/body/eval_jaxpr/ppermute | solution.py:12
  274.4 8.2 %collective-permute-done = f32[2,128,128]{2,1,0:T(8,128)S(1)} collective-permute-done((f32[2,128,128]{2,1,0:T(8,128)S(1)}, f32[2,128,128]{2,1,0:T(8,128)S(1)}, u32[]{:S(2)}, u32[]{:S(2)}) %collective-permute-start) | collective-permute-done | bytes 131104 | tf_op jit(solution)/shard_map/while/body/eval_jaxpr/ppermute | solution.py:12
  284.8 7.6 %collective-permute-done = f32[2,128,128]{2,1,0:T(8,128)S(1)} collective-permute-done((f32[2,128,128]{2,1,0:T(8,128)S(1)}, f32[2,128,128]{2,1,0:T(8,128)S(1)}, u32[]{:S(2)}, u32[]{:S(2)}) %collective-permute-start) | collective-permute-done | bytes 131104 | tf_op jit(solution)/shard_map/while/body/eval_jaxpr/ppermute | solution.py:12
  294.7 7.0 %collective-permute-done = f32[2,128,128]{2,1,0:T(8,128)S(1)} collective-permute-done((f32[2,128,128]{2,1,0:T(8,128)S(1)}, f32[2,128,128]{2,1,0:T(8,128)S(1)}, u32[]{:S(2)}, u32[]{:S(2)}) %collective-permute-start) | collective-permute-done | bytes 131104 | tf_op jit(solution)/shard_map/while/body/eval_jaxpr/ppermute | solution.py:12
  303.9 7.0 %collective-permute-done = f32[2,128,128]{2,1,0:T(8,128)S(1)} collective-permute-done((f32[2,128,128]{2,1,0:T(8,128)S(1)}, f32[2,128,128]{2,1,0:T(8,128)S(1)}, u32[]{:S(2)}, u32[]{:S(2)}) %collective-permute-start) | collective-permute-done | bytes 131104 | tf_op jit(solution)/shard_map/while/body/eval_jaxpr/ppermute | solution.py:12
  313.2 7.0 %collective-permute-done = f32[2,128,128]{2,1,0:T(8,128)S(1)} collective-permute-done((f32[2,128,128]{2,1,0:T(8,128)S(1)}, f32[2,128,128]{2,1,0:T(8,128)S(1)}, u32[]{:S(2)}, u32[]{:S(2)}) %collective-permute-start) | collective-permute-done | bytes 131104 | tf_op jit(solution)/shard_map/while/body/eval_jaxpr/ppermute | solution.py:12
  322.5 7.0 %collective-permute-done = f32[2,128,128]{2,1,0:T(8,128)S(1)} collective-permute-done((f32[2,128,128]{2,1,0:T(8,128)S(1)}, f32[2,128,128]{2,1,0:T(8,128)S(1)}, u32[]{:S(2)}, u32[]{:S(2)}) %collective-permute-start) | collective-permute-done | bytes 131104 | tf_op jit(solution)/shard_map/while/body/eval_jaxpr/ppermute | solution.py:12
  331.8 7.0 %collective-permute-done = f32[2,128,128]{2,1,0:T(8,128)S(1)} collective-permute-done((f32[2,128,128]{2,1,0:T(8,128)S(1)}, f32[2,128,128]{2,1,0:T(8,128)S(1)}, u32[]{:S(2)}, u32[]{:S(2)}) %collective-permute-start) | collective-permute-done | bytes 131104 | tf_op jit(solution)/shard_map/while/body/eval_jaxpr/ppermute | solution.py:12
  341.1 7.8 %collective-permute-done = f32[2,128,128]{2,1,0:T(8,128)S(1)} collective-permute-done((f32[2,128,128]{2,1,0:T(8,128)S(1)}, f32[2,128,128]{2,1,0:T(8,128)S(1)}, u32[]{:S(2)}, u32[]{:S(2)}) %collective-permute-start) | collective-permute-done | bytes 131104 | tf_op jit(solution)/shard_map/while/body/eval_jaxpr/ppermute | solution.py:12
  351.1 8.0 %collective-permute-done = f32[2,128,128]{2,1,0:T(8,128)S(1)} collective-permute-done((f32[2,128,128]{2,1,0:T(8,128)S(1)}, f32[2,128,128]{2,1,0:T(8,128)S(1)}, u32[]{:S(2)}, u32[]{:S(2)}) %collective-permute-start) | collective-permute-done | bytes 131104 | tf_op jit(solution)/shard_map/while/body/eval_jaxpr/ppermute | solution.py:12
  361.3 7.2 %collective-permute-done = f32[2,128,128]{2,1,0:T(8,128)S(1)} collective-permute-done((f32[2,128,128]{2,1,0:T(8,128)S(1)}, f32[2,128,128]{2,1,0:T(8,128)S(1)}, u32[]{:S(2)}, u32[]{:S(2)}) %collective-permute-start) | collective-permute-done | bytes 131104 | tf_op jit(solution)/shard_map/while/body/eval_jaxpr/ppermute | solution.py:12
  370.7 7.0 %collective-permute-done = f32[2,128,128]{2,1,0:T(8,128)S(1)} collective-permute-done((f32[2,128,128]{2,1,0:T(8,128)S(1)}, f32[2,128,128]{2,1,0:T(8,128)S(1)}, u32[]{:S(2)}, u32[]{:S(2)}) %collective-permute-start) | collective-permute-done | bytes 131104 | tf_op jit(solution)/shard_map/while/body/eval_jaxpr/ppermute | solution.py:12
  380.0 7.0 %collective-permute-done = f32[2,128,128]{2,1,0:T(8,128)S(1)} collective-permute-done((f32[2,128,128]{2,1,0:T(8,128)S(1)}, f32[2,128,128]{2,1,0:T(8,128)S(1)}, u32[]{:S(2)}, u32[]{:S(2)}) %collective-permute-start) | collective-permute-done | bytes 131104 | tf_op jit(solution)/shard_map/while/body/eval_jaxpr/ppermute | solution.py:12
  389.2 7.0 %collective-permute-done = f32[2,128,128]{2,1,0:T(8,128)S(1)} collective-permute-done((f32[2,128,128]{2,1,0:T(8,128)S(1)}, f32[2,128,128]{2,1,0:T(8,128)S(1)}, u32[]{:S(2)}, u32[]{:S(2)}) %collective-permute-start) | collective-permute-done | bytes 131104 | tf_op jit(solution)/shard_map/while/body/eval_jaxpr/ppermute | solution.py:12
  398.5 7.0 %collective-permute-done = f32[2,128,128]{2,1,0:T(8,128)S(1)} collective-permute-done((f32[2,128,128]{2,1,0:T(8,128)S(1)}, f32[2,128,128]{2,1,0:T(8,128)S(1)}, u32[]{:S(2)}, u32[]{:S(2)}) %collective-permute-start) | collective-permute-done | bytes 131104 | tf_op jit(solution)/shard_map/while/body/eval_jaxpr/ppermute | solution.py:12
  433.4 103.2 %while.39 = (s32[]{:T(128)}, f32[2,128,128]{2,1,0:T(8,128)S(1)}, f32[32,2,16,128]{3,2,1,0:T(8,128)}, f32[32,2,16,128]{3,2,1,0:T(8,128)S(1)}, f32[32,2,16]{2,1,0:...) while((s32[]{:T(128)}, f32[2,128,128]{2,1,0:T(8,128)S(1)}, ...), condition=%wide.region_7.8_spmd.clone, body=%wide.region_6.7_spmd.clone.sunk | while | flops 20493824 | bytes 770417 | solution.py:80
  543.4 35.3 %reduce-scatter.2.cloned.1.call-done = bf16[512,512]{1,0:T(8,128)(2,1)} async-done(((bf16[512,4096]{1,0:T(8,128)(2,1)}), bf16[512,512]{1,0:T(8,128)(2,1)}) %reduce-scatter.2.cloned.1.call-update) | async-done | bytes 524304 | tf_op jit(solution)/shard_map/reduce_scatter | solution.py:85
  (556 shorter events, 299.8 us)
Async XLA Ops:
  6.5 40.3 %all-gather.2.cloned.1.call-start = ((), (), s32[]{:S(2)}) async-start(), calls=%async_computation.1 | async-start | bytes 4718592 | tf_op jit(solution)/shard_map/all_gather | solution.py:35
  7.3 571.5 %reduce-scatter.2.cloned.1.call-start = ((), (), s32[]{:S(2)}) async-start(), calls=%async_computation.2 | async-start | bytes 4718592 | tf_op jit(solution)/shard_map/reduce_scatter | solution.py:85
  140.0 9.7 %collective-permute-start = (f32[2,128,128]{2,1,0:T(8,128)S(1)}, f32[2,128,128]{2,1,0:T(8,128)S(1)}, u32[]{:S(2)}, u32[]{:S(2)}) collective-permute-start(f32[2,128,128]{2,1,0:T(8,128)S(1)} %convolution_add_fusion.2), channel_id=1, source_target_pairs={{0,8},{8,16},{16,24},{24,32},{32,40},{40,48},{48,56},{56,64},{64,7... | collective-permute-start | bytes 393224 | tf_op jit(solution)/shard_map/while/body/eval_jaxpr/ppermute | solution.py:12
  149.9 9.0 %collective-permute-start = (f32[2,128,128]{2,1,0:T(8,128)S(1)}, f32[2,128,128]{2,1,0:T(8,128)S(1)}, u32[]{:S(2)}, u32[]{:S(2)}) collective-permute-start(f32[2,128,128]{2,1,0:T(8,128)S(1)} %convolution_add_fusion.2), channel_id=1, source_target_pairs={{0,8},{8,16},{16,24},{24,32},{32,40},{40,48},{48,56},{56,64},{64,7... | collective-permute-start | bytes 393224 | tf_op jit(solution)/shard_map/while/body/eval_jaxpr/ppermute | solution.py:12
  159.2 9.0 %collective-permute-start = (f32[2,128,128]{2,1,0:T(8,128)S(1)}, f32[2,128,128]{2,1,0:T(8,128)S(1)}, u32[]{:S(2)}, u32[]{:S(2)}) collective-permute-start(f32[2,128,128]{2,1,0:T(8,128)S(1)} %convolution_add_fusion.2), channel_id=1, source_target_pairs={{0,8},{8,16},{16,24},{24,32},{32,40},{40,48},{48,56},{56,64},{64,7... | collective-permute-start | bytes 393224 | tf_op jit(solution)/shard_map/while/body/eval_jaxpr/ppermute | solution.py:12
  168.5 9.0 %collective-permute-start = (f32[2,128,128]{2,1,0:T(8,128)S(1)}, f32[2,128,128]{2,1,0:T(8,128)S(1)}, u32[]{:S(2)}, u32[]{:S(2)}) collective-permute-start(f32[2,128,128]{2,1,0:T(8,128)S(1)} %convolution_add_fusion.2), channel_id=1, source_target_pairs={{0,8},{8,16},{16,24},{24,32},{32,40},{40,48},{48,56},{56,64},{64,7... | collective-permute-start | bytes 393224 | tf_op jit(solution)/shard_map/while/body/eval_jaxpr/ppermute | solution.py:12
  177.8 9.0 %collective-permute-start = (f32[2,128,128]{2,1,0:T(8,128)S(1)}, f32[2,128,128]{2,1,0:T(8,128)S(1)}, u32[]{:S(2)}, u32[]{:S(2)}) collective-permute-start(f32[2,128,128]{2,1,0:T(8,128)S(1)} %convolution_add_fusion.2), channel_id=1, source_target_pairs={{0,8},{8,16},{16,24},{24,32},{32,40},{40,48},{48,56},{56,64},{64,7... | collective-permute-start | bytes 393224 | tf_op jit(solution)/shard_map/while/body/eval_jaxpr/ppermute | solution.py:12
  187.0 9.0 %collective-permute-start = (f32[2,128,128]{2,1,0:T(8,128)S(1)}, f32[2,128,128]{2,1,0:T(8,128)S(1)}, u32[]{:S(2)}, u32[]{:S(2)}) collective-permute-start(f32[2,128,128]{2,1,0:T(8,128)S(1)} %convolution_add_fusion.2), channel_id=1, source_target_pairs={{0,8},{8,16},{16,24},{24,32},{32,40},{40,48},{48,56},{56,64},{64,7... | collective-permute-start | bytes 393224 | tf_op jit(solution)/shard_map/while/body/eval_jaxpr/ppermute | solution.py:12
  196.3 9.5 %collective-permute-start = (f32[2,128,128]{2,1,0:T(8,128)S(1)}, f32[2,128,128]{2,1,0:T(8,128)S(1)}, u32[]{:S(2)}, u32[]{:S(2)}) collective-permute-start(f32[2,128,128]{2,1,0:T(8,128)S(1)} %convolution_add_fusion.2), channel_id=1, source_target_pairs={{0,8},{8,16},{16,24},{24,32},{32,40},{40,48},{48,56},{56,64},{64,7... | collective-permute-start | bytes 393224 | tf_op jit(solution)/shard_map/while/body/eval_jaxpr/ppermute | solution.py:12
  206.2 10.1 %collective-permute-start = (f32[2,128,128]{2,1,0:T(8,128)S(1)}, f32[2,128,128]{2,1,0:T(8,128)S(1)}, u32[]{:S(2)}, u32[]{:S(2)}) collective-permute-start(f32[2,128,128]{2,1,0:T(8,128)S(1)} %convolution_add_fusion.2), channel_id=1, source_target_pairs={{0,8},{8,16},{16,24},{24,32},{32,40},{40,48},{48,56},{56,64},{64,7... | collective-permute-start | bytes 393224 | tf_op jit(solution)/shard_map/while/body/eval_jaxpr/ppermute | solution.py:12
  216.5 9.2 %collective-permute-start = (f32[2,128,128]{2,1,0:T(8,128)S(1)}, f32[2,128,128]{2,1,0:T(8,128)S(1)}, u32[]{:S(2)}, u32[]{:S(2)}) collective-permute-start(f32[2,128,128]{2,1,0:T(8,128)S(1)} %convolution_add_fusion.2), channel_id=1, source_target_pairs={{0,8},{8,16},{16,24},{24,32},{32,40},{40,48},{48,56},{56,64},{64,7... | collective-permute-start | bytes 393224 | tf_op jit(solution)/shard_map/while/body/eval_jaxpr/ppermute | solution.py:12
  226.1 9.0 %collective-permute-start = (f32[2,128,128]{2,1,0:T(8,128)S(1)}, f32[2,128,128]{2,1,0:T(8,128)S(1)}, u32[]{:S(2)}, u32[]{:S(2)}) collective-permute-start(f32[2,128,128]{2,1,0:T(8,128)S(1)} %convolution_add_fusion.2), channel_id=1, source_target_pairs={{0,8},{8,16},{16,24},{24,32},{32,40},{40,48},{48,56},{56,64},{64,7... | collective-permute-start | bytes 393224 | tf_op jit(solution)/shard_map/while/body/eval_jaxpr/ppermute | solution.py:12
  235.3 9.0 %collective-permute-start = (f32[2,128,128]{2,1,0:T(8,128)S(1)}, f32[2,128,128]{2,1,0:T(8,128)S(1)}, u32[]{:S(2)}, u32[]{:S(2)}) collective-permute-start(f32[2,128,128]{2,1,0:T(8,128)S(1)} %convolution_add_fusion.2), channel_id=1, source_target_pairs={{0,8},{8,16},{16,24},{24,32},{32,40},{40,48},{48,56},{56,64},{64,7... | collective-permute-start | bytes 393224 | tf_op jit(solution)/shard_map/while/body/eval_jaxpr/ppermute | solution.py:12
  244.6 9.0 %collective-permute-start = (f32[2,128,128]{2,1,0:T(8,128)S(1)}, f32[2,128,128]{2,1,0:T(8,128)S(1)}, u32[]{:S(2)}, u32[]{:S(2)}) collective-permute-start(f32[2,128,128]{2,1,0:T(8,128)S(1)} %convolution_add_fusion.2), channel_id=1, source_target_pairs={{0,8},{8,16},{16,24},{24,32},{32,40},{40,48},{48,56},{56,64},{64,7... | collective-permute-start | bytes 393224 | tf_op jit(solution)/shard_map/while/body/eval_jaxpr/ppermute | solution.py:12
  253.9 9.0 %collective-permute-start = (f32[2,128,128]{2,1,0:T(8,128)S(1)}, f32[2,128,128]{2,1,0:T(8,128)S(1)}, u32[]{:S(2)}, u32[]{:S(2)}) collective-permute-start(f32[2,128,128]{2,1,0:T(8,128)S(1)} %convolution_add_fusion.2), channel_id=1, source_target_pairs={{0,8},{8,16},{16,24},{24,32},{32,40},{40,48},{48,56},{56,64},{64,7... | collective-permute-start | bytes 393224 | tf_op jit(solution)/shard_map/while/body/eval_jaxpr/ppermute | solution.py:12
  263.2 9.0 %collective-permute-start = (f32[2,128,128]{2,1,0:T(8,128)S(1)}, f32[2,128,128]{2,1,0:T(8,128)S(1)}, u32[]{:S(2)}, u32[]{:S(2)}) collective-permute-start(f32[2,128,128]{2,1,0:T(8,128)S(1)} %convolution_add_fusion.2), channel_id=1, source_target_pairs={{0,8},{8,16},{16,24},{24,32},{32,40},{40,48},{48,56},{56,64},{64,7... | collective-permute-start | bytes 393224 | tf_op jit(solution)/shard_map/while/body/eval_jaxpr/ppermute | solution.py:12
  272.5 10.1 %collective-permute-start = (f32[2,128,128]{2,1,0:T(8,128)S(1)}, f32[2,128,128]{2,1,0:T(8,128)S(1)}, u32[]{:S(2)}, u32[]{:S(2)}) collective-permute-start(f32[2,128,128]{2,1,0:T(8,128)S(1)} %convolution_add_fusion.2), channel_id=1, source_target_pairs={{0,8},{8,16},{16,24},{24,32},{32,40},{40,48},{48,56},{56,64},{64,7... | collective-permute-start | bytes 393224 | tf_op jit(solution)/shard_map/while/body/eval_jaxpr/ppermute | solution.py:12
  282.9 9.5 %collective-permute-start = (f32[2,128,128]{2,1,0:T(8,128)S(1)}, f32[2,128,128]{2,1,0:T(8,128)S(1)}, u32[]{:S(2)}, u32[]{:S(2)}) collective-permute-start(f32[2,128,128]{2,1,0:T(8,128)S(1)} %convolution_add_fusion.2), channel_id=1, source_target_pairs={{0,8},{8,16},{16,24},{24,32},{32,40},{40,48},{48,56},{56,64},{64,7... | collective-permute-start | bytes 393224 | tf_op jit(solution)/shard_map/while/body/eval_jaxpr/ppermute | solution.py:12
  292.7 9.0 %collective-permute-start = (f32[2,128,128]{2,1,0:T(8,128)S(1)}, f32[2,128,128]{2,1,0:T(8,128)S(1)}, u32[]{:S(2)}, u32[]{:S(2)}) collective-permute-start(f32[2,128,128]{2,1,0:T(8,128)S(1)} %convolution_add_fusion.2), channel_id=1, source_target_pairs={{0,8},{8,16},{16,24},{24,32},{32,40},{40,48},{48,56},{56,64},{64,7... | collective-permute-start | bytes 393224 | tf_op jit(solution)/shard_map/while/body/eval_jaxpr/ppermute | solution.py:12
  302.0 9.0 %collective-permute-start = (f32[2,128,128]{2,1,0:T(8,128)S(1)}, f32[2,128,128]{2,1,0:T(8,128)S(1)}, u32[]{:S(2)}, u32[]{:S(2)}) collective-permute-start(f32[2,128,128]{2,1,0:T(8,128)S(1)} %convolution_add_fusion.2), channel_id=1, source_target_pairs={{0,8},{8,16},{16,24},{24,32},{32,40},{40,48},{48,56},{56,64},{64,7... | collective-permute-start | bytes 393224 | tf_op jit(solution)/shard_map/while/body/eval_jaxpr/ppermute | solution.py:12
  311.3 9.0 %collective-permute-start = (f32[2,128,128]{2,1,0:T(8,128)S(1)}, f32[2,128,128]{2,1,0:T(8,128)S(1)}, u32[]{:S(2)}, u32[]{:S(2)}) collective-permute-start(f32[2,128,128]{2,1,0:T(8,128)S(1)} %convolution_add_fusion.2), channel_id=1, source_target_pairs={{0,8},{8,16},{16,24},{24,32},{32,40},{40,48},{48,56},{56,64},{64,7... | collective-permute-start | bytes 393224 | tf_op jit(solution)/shard_map/while/body/eval_jaxpr/ppermute | solution.py:12
  320.6 9.0 %collective-permute-start = (f32[2,128,128]{2,1,0:T(8,128)S(1)}, f32[2,128,128]{2,1,0:T(8,128)S(1)}, u32[]{:S(2)}, u32[]{:S(2)}) collective-permute-start(f32[2,128,128]{2,1,0:T(8,128)S(1)} %convolution_add_fusion.2), channel_id=1, source_target_pairs={{0,8},{8,16},{16,24},{24,32},{32,40},{40,48},{48,56},{56,64},{64,7... | collective-permute-start | bytes 393224 | tf_op jit(solution)/shard_map/while/body/eval_jaxpr/ppermute | solution.py:12
  329.8 9.0 %collective-permute-start = (f32[2,128,128]{2,1,0:T(8,128)S(1)}, f32[2,128,128]{2,1,0:T(8,128)S(1)}, u32[]{:S(2)}, u32[]{:S(2)}) collective-permute-start(f32[2,128,128]{2,1,0:T(8,128)S(1)} %convolution_add_fusion.2), channel_id=1, source_target_pairs={{0,8},{8,16},{16,24},{24,32},{32,40},{40,48},{48,56},{56,64},{64,7... | collective-permute-start | bytes 393224 | tf_op jit(solution)/shard_map/while/body/eval_jaxpr/ppermute | solution.py:12
  339.1 9.7 %collective-permute-start = (f32[2,128,128]{2,1,0:T(8,128)S(1)}, f32[2,128,128]{2,1,0:T(8,128)S(1)}, u32[]{:S(2)}, u32[]{:S(2)}) collective-permute-start(f32[2,128,128]{2,1,0:T(8,128)S(1)} %convolution_add_fusion.2), channel_id=1, source_target_pairs={{0,8},{8,16},{16,24},{24,32},{32,40},{40,48},{48,56},{56,64},{64,7... | collective-permute-start | bytes 393224 | tf_op jit(solution)/shard_map/while/body/eval_jaxpr/ppermute | solution.py:12
  349.2 9.9 %collective-permute-start = (f32[2,128,128]{2,1,0:T(8,128)S(1)}, f32[2,128,128]{2,1,0:T(8,128)S(1)}, u32[]{:S(2)}, u32[]{:S(2)}) collective-permute-start(f32[2,128,128]{2,1,0:T(8,128)S(1)} %convolution_add_fusion.2), channel_id=1, source_target_pairs={{0,8},{8,16},{16,24},{24,32},{32,40},{40,48},{48,56},{56,64},{64,7... | collective-permute-start | bytes 393224 | tf_op jit(solution)/shard_map/while/body/eval_jaxpr/ppermute | solution.py:12
  359.3 9.1 %collective-permute-start = (f32[2,128,128]{2,1,0:T(8,128)S(1)}, f32[2,128,128]{2,1,0:T(8,128)S(1)}, u32[]{:S(2)}, u32[]{:S(2)}) collective-permute-start(f32[2,128,128]{2,1,0:T(8,128)S(1)} %convolution_add_fusion.2), channel_id=1, source_target_pairs={{0,8},{8,16},{16,24},{24,32},{32,40},{40,48},{48,56},{56,64},{64,7... | collective-permute-start | bytes 393224 | tf_op jit(solution)/shard_map/while/body/eval_jaxpr/ppermute | solution.py:12
  368.8 9.0 %collective-permute-start = (f32[2,128,128]{2,1,0:T(8,128)S(1)}, f32[2,128,128]{2,1,0:T(8,128)S(1)}, u32[]{:S(2)}, u32[]{:S(2)}) collective-permute-start(f32[2,128,128]{2,1,0:T(8,128)S(1)} %convolution_add_fusion.2), channel_id=1, source_target_pairs={{0,8},{8,16},{16,24},{24,32},{32,40},{40,48},{48,56},{56,64},{64,7... | collective-permute-start | bytes 393224 | tf_op jit(solution)/shard_map/while/body/eval_jaxpr/ppermute | solution.py:12
  378.0 9.0 %collective-permute-start = (f32[2,128,128]{2,1,0:T(8,128)S(1)}, f32[2,128,128]{2,1,0:T(8,128)S(1)}, u32[]{:S(2)}, u32[]{:S(2)}) collective-permute-start(f32[2,128,128]{2,1,0:T(8,128)S(1)} %convolution_add_fusion.2), channel_id=1, source_target_pairs={{0,8},{8,16},{16,24},{24,32},{32,40},{40,48},{48,56},{56,64},{64,7... | collective-permute-start | bytes 393224 | tf_op jit(solution)/shard_map/while/body/eval_jaxpr/ppermute | solution.py:12
  387.3 9.0 %collective-permute-start = (f32[2,128,128]{2,1,0:T(8,128)S(1)}, f32[2,128,128]{2,1,0:T(8,128)S(1)}, u32[]{:S(2)}, u32[]{:S(2)}) collective-permute-start(f32[2,128,128]{2,1,0:T(8,128)S(1)} %convolution_add_fusion.2), channel_id=1, source_target_pairs={{0,8},{8,16},{16,24},{24,32},{32,40},{40,48},{48,56},{56,64},{64,7... | collective-permute-start | bytes 393224 | tf_op jit(solution)/shard_map/while/body/eval_jaxpr/ppermute | solution.py:12
  396.6 9.0 %collective-permute-start = (f32[2,128,128]{2,1,0:T(8,128)S(1)}, f32[2,128,128]{2,1,0:T(8,128)S(1)}, u32[]{:S(2)}, u32[]{:S(2)}) collective-permute-start(f32[2,128,128]{2,1,0:T(8,128)S(1)} %convolution_add_fusion.2), channel_id=1, source_target_pairs={{0,8},{8,16},{16,24},{24,32},{32,40},{40,48},{48,56},{56,64},{64,7... | collective-permute-start | bytes 393224 | tf_op jit(solution)/shard_map/while/body/eval_jaxpr/ppermute | solution.py:12
  405.9 9.0 %collective-permute-start = (f32[2,128,128]{2,1,0:T(8,128)S(1)}, f32[2,128,128]{2,1,0:T(8,128)S(1)}, u32[]{:S(2)}, u32[]{:S(2)}) collective-permute-start(f32[2,128,128]{2,1,0:T(8,128)S(1)} %convolution_add_fusion.2), channel_id=1, source_target_pairs={{0,8},{8,16},{16,24},{24,32},{32,40},{40,48},{48,56},{56,64},{64,7... | collective-permute-start | bytes 393224 | tf_op jit(solution)/shard_map/while/body/eval_jaxpr/ppermute | solution.py:12
  415.2 9.0 %collective-permute-start = (f32[2,128,128]{2,1,0:T(8,128)S(1)}, f32[2,128,128]{2,1,0:T(8,128)S(1)}, u32[]{:S(2)}, u32[]{:S(2)}) collective-permute-start(f32[2,128,128]{2,1,0:T(8,128)S(1)} %convolution_add_fusion.2), channel_id=1, source_target_pairs={{0,8},{8,16},{16,24},{24,32},{32,40},{40,48},{48,56},{56,64},{64,7... | collective-permute-start | bytes 393224 | tf_op jit(solution)/shard_map/while/body/eval_jaxpr/ppermute | solution.py:12
  (4 other events, 718.3 us)
Sparse Core Ops, SparseCore 0:
  9.2 37.6 all-gather.1
  543.5 35.1 reduce-scatter.1
where the time goes:
time: 596 us; the launch traced here: 586 us
  waiting for transfers between devices  298 us (50%)
  matrix products  165 us (28%)
  starting transfers between devices  61.1 us (10%)
  local copies, waits for them, and re-layouts  37.4 us (6%)
  between operations  13.6 us (2%)
  other arithmetic  8.61 us (1%)
    ppermute x31, waiting for transfers between devices, from_behind(): return lax.ppermute(block, axis, route)  223 us
    dot_general x319, matrix products, mm(): return jnp.einsum(form, a, b, precision=lax.Precision.HIGHEST)  151 us
    ppermute x31, starting transfers between devices, from_behind(): return lax.ppermute(block, axis, route)  61.1 us
    all_gather x1, waiting for transfers between devices, local(): piece = lax.all_gather(hidden_in, 'tp', axis=1, tiled=True)  38.6 us
    reduce_scatter x1, waiting for transfers between devices, local(): lax.psum_scatter(terms.astype(jnp.bfloat16), 'tp', scatter_dimension=1, t...  35.3 us
    dynamic_slice x32, local copies, waits for them, and re-layouts, local(): lax.scan(gather_map_step, (identity_map, zero_map), (keys, values, rate_b...  23 us
  transfers between devices with their start and end apart: 33, of which 33 were waited for; matrix products, arithmetic and copies ran while one was open for 0% of the time, Pallas kernels for 0%

commit v1 on v0

v1 whole, which is shorter than its diff:
```python
import jax
import jax.numpy as jnp
from jax import lax
from jax.experimental import pallas as pl
from jax.experimental.pallas import tpu as pltpu
from jax.sharding import PartitionSpec as P

MB = 16
CH = 128
MESH = pl.DeviceIdType.MESH
F32 = jnp.float32
BF16 = jnp.bfloat16
Y, CORES = 4, 2
X, Z = 4, 8


def dot(a, b):
    return jnp.dot(a.astype(BF16), b.astype(BF16), preferred_element_type=F32)


def compose(later, earlier, hd):
    return earlier + dot(later[:, :hd], earlier) + later


def apply_map(m, w, hd):
    return w + dot(m[:, :hd], w) + m[:, hd:]


def gather_kernel(hid, wq, lrw, lr, p_out, n_out, x_out, xg, wbuf, lrt, pref, loc, send, recv, wsem):
    rows, feat = hid.shape
    nc = rows // CH
    half = CH // 2
    hd = x_out.shape[1]
    heads = x_out.shape[0]
    width = heads * hd
    me = lax.axis_index("tp")
    ring = Y * CORES
    sib = me + 1 - 2 * lax.rem(me, 2)
    up = lax.rem(me + 2, ring)
    down = lax.rem(me + ring - 2, ring)
    opp = lax.rem(me + 4, ring)

    barrier = pltpu.get_barrier_semaphore()
    for peer in (sib, up, down):
        pl.semaphore_signal(barrier, inc=1, device_id={"tp": peer}, device_id_type=MESH)

    wcopies = [
        pltpu.make_async_copy(wq.at[c], wbuf.at[:, pl.ds(c * width, width)], wsem.at[c]) for c in range(3)
    ]
    for cp in wcopies:
        cp.start()

    def cols(j):
        return pl.ds(pl.multiple_of(j * feat, feat), feat)

    def transfer(kind, c):
        if kind < 3:
            src, r0, n, owner = hid, 0, CH, me
        elif kind in (3, 5):
            src, r0, n, owner = xg, 0, (half if kind == 3 else CH), down
        elif kind in (4, 6):
            src, r0, n, owner = xg, (half if kind == 4 else 0), (half if kind == 4 else CH), up
        else:
            src, r0, n, owner = xg, (0 if kind == 7 else half), half, opp
        to = {0: up, 1: down, 3: up, 4: down}.get(kind, sib)
        rs = pl.ds(pl.multiple_of(c * CH + r0, 16), n)
        source = hid.at[rs] if kind < 3 else xg.at[rs, cols(owner)]
        return pltpu.make_async_remote_copy(
            src_ref=source,
            dst_ref=xg.at[rs, cols(owner)],
            send_sem=send.at[c, kind],
            recv_sem=recv.at[c, kind],
            device_id={"tp": to},
            device_id_type=MESH,
        )

    def arrival(kind, c):
        owner = {0: down, 1: up, 2: sib, 3: opp, 4: opp, 5: lax.rem(sib + ring - 2, ring),
                 6: lax.rem(sib + 2, ring), 7: lax.rem(sib + 4, ring), 8: lax.rem(sib + 4, ring)}[kind]
        r0 = half if kind in (4, 8) else 0
        n = half if kind in (3, 4, 7, 8) else CH
        rs = pl.ds(pl.multiple_of(c * CH + r0, 16), n)
        dst = xg.at[rs, cols(owner)]
        return pltpu.make_async_remote_copy(
            src_ref=dst, dst_ref=dst, send_sem=send.at[c, kind], recv_sem=recv.at[c, kind],
            device_id={"tp": sib}, device_id_type=MESH,
        )

    def begin(c):
        for kind in range(3):
            transfer(kind, c).start()

    def forward(c):
        arrival(0, c).wait_recv()
        transfer(3, c).start()
        transfer(5, c).start()
        arrival(1, c).wait_recv()
        transfer(4, c).start()
        transfer(6, c).start()

    def forward_opposite(c):
        arrival(3, c).wait_recv()
        transfer(7, c).start()
        arrival(4, c).wait_recv()
        transfer(8, c).start()

    pl.semaphore_wait(barrier, 3)
    begin(0)
    begin(1)
    own = pltpu.make_async_copy(hid, xg.at[:, cols(me)], loc)
    own.start()

    lrt[...] = jnp.zeros_like(lrt)
    lrt[0:heads, :] = lrw[...].astype(F32)
    for i in range(wbuf.shape[0] // CH):
        wbuf[i * CH:(i + 1) * CH, 3 * width:] = lrt[:, i * CH:(i + 1) * CH].T.astype(BF16)
    pref[...] = jnp.zeros_like(pref)
    own.wait()
    forward(0)
    forward_opposite(0)
    for cp in wcopies:
        cp.wait()

    row = lax.broadcasted_iota(jnp.int32, (CH, CH), 0)
    col = lax.broadcasted_iota(jnp.int32, (CH, CH), 1)
    causal = row >= col
    before = (row >> 4) > (col >> 4)

    def chunk(c, carry):
        @pl.when(c < nc - 2)
        def _():
            begin(c + 2)

        @pl.when(c < nc - 1)
        def _():
            forward(c + 1)

        for kind in (2, 5, 6, 7, 8):
            arrival(kind, c).wait_recv()
        rs = pl.ds(pl.multiple_of(c * CH, CH), CH)
        proj = jnp.dot(xg[rs, :], wbuf[...], preferred_element_type=F32)

        @pl.when(c < nc - 1)
        def _():
            forward_opposite(c + 1)

        hs = range(heads)
        part = [[proj[:, (k * heads + h) * hd:(k * heads + h + 1) * hd] for h in hs] for k in range(3)]

        def unit(v):
            return v * lax.rsqrt(jnp.sum(v * v, -1, keepdims=True) + hd * 1e-06)

        q = [unit(part[0][h]) for h in hs]
        k = [unit(part[1][h]) for h in hs]
        rate = [lr[h] * jax.nn.sigmoid(proj[:, 3 * width + h:3 * width + h + 1]) for h in hs]
        krt = [(k[h] * rate[h]).T.astype(BF16) for h in hs]
        sg = [dot(jnp.concatenate([q[h], k[h]], 0), krt[h]) for h in hs]
        m = [jnp.where(causal, sg[h][:CH], 0.0).astype(BF16) for h in hs]
        l1 = [jnp.where(before, sg[h][CH:], 0.0) for h in hs]
        lb = [l1[h].astype(BF16) for h in hs]
        l2 = [dot(lb[h], lb[h]) for h in hs]
        l34 = [dot(jnp.concatenate([lb[h], l2[h].astype(BF16)], 0), l2[h]) for h in hs]
        t1 = [l2[h] - l1[h] - l34[h][:CH] for h in hs]
        t = [t1[h] + l34[h][CH:] + dot(t1[h], l34[h][CH:]) for h in hs]
        kv = [jnp.concatenate([k[h], part[2][h]], 1) for h in hs]
        uy = [kv[h] + dot(t[h], kv[h]) for h in hs]
        dn = [dot(jnp.concatenate([krt[h], m[h]], 0), uy[h]) for h in hs]
        d = [jnp.concatenate([-dn[h][:CH, :hd], dn[h][:CH, hd:]], 1) for h in hs]
        p = [q[h] - dn[h][CH:, :hd] for h in hs]
        n = [dn[h][CH:, hd:] for h in hs]
        x0 = [pref[h] for h in hs]
        dx = [dot(jnp.concatenate([d[h][:, :hd], p[h]], 0), x0[h]) for h in hs]
        for h in hs:
            pref[h] = x0[h] + dx[h][:CH] + d[h]
            p_out[rs, h * hd:(h + 1) * hd] = (p[h] + dx[h][CH:, :hd]).astype(BF16)
            n_out[rs, h * hd:(h + 1) * hd] = n[h] + dx[h][CH:, hd:]
        return carry

    lax.fori_loop(0, nc, chunk, 0)
    x_out[...] = pref[...].astype(BF16)

    def drain(c, carry):
        for kind in range(9):
            transfer(kind, c).wait_send()
        return carry

    lax.fori_loop(0, nc, drain, 0)


def scan_kernel(p_in, n_in, x_in, w0, gain, normed, maps, pairs, quads, prefix, totals, wst, rsend, rrecv, lsend, lrecv, xsend, xrecv):
    heads, hd = x_in.shape[0], x_in.shape[1]
    me = lax.axis_index("ctx")
    z = lax.rem(me, Z)
    x = me // Z
    base = x * Z
    right = base + lax.rem(z + 1, Z)
    left = base + lax.rem(z + Z - 1, Z)

    barrier = pltpu.get_barrier_semaphore()
    for peer in (right, left):
        pl.semaphore_signal(barrier, inc=1, device_id={"ctx": peer}, device_id_type=MESH)
    for d in range(1, X):
        pl.semaphore_signal(
            barrier, inc=1, device_id={"ctx": lax.rem(me + d * Z, X * Z)}, device_id_type=MESH
        )
    maps[z] = x_in[...]
    pl.semaphore_wait(barrier, 2 + X - 1)

    def slot(distance):
        return lax.rem(z + distance + Z, Z)

    reach = {"r": (4, 3), "l": (3, 4)}

    def hop(way, h, s, arriving):
        sign = -1 if way == "r" else 1
        ref = maps.at[slot(sign * (s + 1 if arriving else s)), h]
        ss, rr = (rsend, rrecv) if way == "r" else (lsend, lrecv)
        return pltpu.make_async_remote_copy(
            src_ref=ref, dst_ref=ref, send_sem=ss.at[h, s], recv_sem=rr.at[h, s],
            device_id={"ctx": right if way == "r" else left}, device_id_type=MESH,
        )

    for s in range(4):
        for h in range(heads):
            for way in ("r", "l"):
                if s < reach[way][h]:
                    if s > 0:
                        hop(way, h, s - 1, True).wait_recv()
                    hop(way, h, s, False).start()

    def to_group(h, d):
        ref = totals.at[x, h]
        return pltpu.make_async_remote_copy(
            src_ref=ref, dst_ref=ref, send_sem=xsend.at[h, d - 1], recv_sem=xrecv.at[h, x],
            device_id={"ctx": lax.rem(me + d * Z, X * Z)}, device_id_type=MESH,
        )

    def from_group(h, j):
        ref = totals.at[j, h]
        return pltpu.make_async_remote_copy(
            src_ref=ref, dst_ref=ref, send_sem=xsend.at[h, 0], recv_sem=xrecv.at[h, j],
            device_id={"ctx": me}, device_id_type=MESH,
        )

    for h in range(heads):
        for way in ("r", "l"):
            hop(way, h, reach[way][h] - 1, True).wait_recv()
        ms = [maps[j, h].astype(F32) for j in range(Z)]
        pr = [compose(ms[2 * j + 1], ms[2 * j], hd) for j in range(Z // 2)]
        qd = [compose(pr[2 * j + 1], pr[2 * j], hd) for j in range(Z // 4)]
        totals[x, h] = compose(qd[1], qd[0], hd).astype(BF16)
        for d in range(1, X):
            @pl.when(x + d < X)
            def _():
                to_group(h, d).start()
        for j in range(Z // 2):
            pairs[h, j] = pr[j]
        quads[h] = qd[0]

    for h in range(heads):
        prefix[h] = jnp.zeros_like(prefix[h])

        @pl.when(z >= 4)
        def _():
            prefix[h] = quads[h]

        @pl.when(lax.rem(z, 4) >= 2)
        def _():
            prefix[h] = compose(pairs[h, z // 2 - 1], prefix[h], hd)

        @pl.when(lax.rem(z, 2) == 1)
        def _():
            prefix[h] = compose(maps[z - 1, h].astype(F32), prefix[h], hd)

        wst[h] = w0[h]
        for j in range(X - 1):
            @pl.when(j < x)
            def _():
                from_group(h, j).wait_recv()
                wst[h] = apply_map(totals[j, h].astype(F32), wst[h], hd)

        w = apply_map(prefix[h], wst[h], hd)
        hc = slice(h * hd, (h + 1) * hd)
        zv = dot(p_in[:, hc], w) + n_in[:, hc]
        zv = zv * lax.rsqrt(jnp.mean(zv * zv, -1, keepdims=True) + 1e-06) * gain[h:h + 1, :]
        normed[:, hc] = zv.astype(BF16)

    for h in range(heads):
        for way in ("r", "l"):
            for s in range(reach[way][h]):
                hop(way, h, s, False).wait_send()
        for d in range(1, X):
            @pl.when(x + d < X)
            def _():
                to_group(h, d).wait_send()


def any_spec():
    return pl.BlockSpec(memory_space=pl.ANY)


def vmem_spec():
    return pl.BlockSpec(memory_space=pltpu.VMEM)


def gather_call(hidden_in, w_qkv, lr_weight, inner_lr):
    rows, feat = hidden_in.shape
    _, depth, width = w_qkv.shape
    heads = inner_lr.shape[0]
    hd = width // heads
    nc = rows // CH
    return pl.pallas_call(
        gather_kernel,
        out_shape=(
            jax.ShapeDtypeStruct((rows, width), BF16),
            jax.ShapeDtypeStruct((rows, width), F32),
            jax.ShapeDtypeStruct((heads, hd, 2 * hd), BF16),
        ),
        in_specs=[any_spec(), any_spec(), vmem_spec(), pl.BlockSpec(memory_space=pltpu.SMEM)],
        out_specs=(vmem_spec(), vmem_spec(), vmem_spec()),
        scratch_shapes=[
            pltpu.VMEM((rows, depth), BF16),
            pltpu.VMEM((depth, 3 * width + CH), BF16),
            pltpu.VMEM((CH, depth), F32),
            pltpu.VMEM((heads, hd, 2 * hd), F32),
            pltpu.SemaphoreType.DMA,
            pltpu.SemaphoreType.DMA((nc, 9)),
            pltpu.SemaphoreType.DMA((nc, 9)),
            pltpu.SemaphoreType.DMA((3,)),
        ],
        compiler_params=pltpu.CompilerParams(
            collective_id=0, has_side_effects=True, vmem_limit_bytes=48 * 1024 * 1024
        ),
        name="gather_maps",
    )(hidden_in, w_qkv, lr_weight.T, inner_lr)


def scan_call(p, n, x, init_state, norm_gain):
    rows, width = p.shape
    heads, hd = norm_gain.shape
    return pl.pallas_call(
        scan_kernel,
        out_shape=jax.ShapeDtypeStruct((rows, width), BF16),
        in_specs=[vmem_spec()] * 5,
        out_specs=vmem_spec(),
        scratch_shapes=[
            pltpu.VMEM((Z, heads, hd, 2 * hd), BF16),
            pltpu.VMEM((heads, Z // 2, hd, 2 * hd), F32),
            pltpu.VMEM((heads, hd, 2 * hd), F32),
            pltpu.VMEM((heads, hd, 2 * hd), F32),
            pltpu.VMEM((X, heads, hd, 2 * hd), BF16),
            pltpu.VMEM((heads, hd, hd), F32),
            pltpu.SemaphoreType.DMA((heads, 4)),
            pltpu.SemaphoreType.DMA((heads, 4)),
            pltpu.SemaphoreType.DMA((heads, 4)),
            pltpu.SemaphoreType.DMA((heads, 4)),
            pltpu.SemaphoreType.DMA((heads, X - 1)),
            pltpu.SemaphoreType.DMA((heads, X)),
        ],
        compiler_params=pltpu.CompilerParams(
            collective_id=1, has_side_effects=True, vmem_limit_bytes=48 * 1024 * 1024
        ),
        name="scan_groups",
    )(p, n, x, init_state, norm_gain)


def local(hidden_in, w_qkv, lr_weight, inner_lr, init_state, norm_gain, w_out):
    tp, ctx = lax.axis_size("tp"), lax.axis_size("ctx")
    share = w_out.shape[0] // ctx
    mine = lax.dynamic_slice_in_dim(w_out, lax.axis_index("ctx") * share, share, 0)
    mine = lax.all_to_all(mine, "tp", split_axis=1, concat_axis=0, tiled=True)
    whole = lax.all_gather(mine, "ctx", axis=0, tiled=True)
    whole = whole.reshape(ctx, tp, share, -1).transpose(1, 0, 2, 3).reshape(ctx * tp * share, -1)
    p, n, x = gather_call(hidden_in, w_qkv, lr_weight, inner_lr)
    normed = scan_call(p, n, x, init_state, norm_gain)
    normed = lax.all_gather(normed, "tp", axis=1, tiled=True)
    return jnp.dot(normed, whole, preferred_element_type=F32).astype(BF16)


def solution(mesh):
    in_specs = (
        P("ctx", "tp"),
        P(None, None, "tp"),
        P(None, "tp"),
        P("tp"),
        P("tp", None, None),
        P("tp", None),
        P("tp", None),
    )
    out_specs = P("ctx", "tp")
    return jax.shard_map(local, mesh=mesh, in_specs=in_specs, out_specs=out_specs, check_vma=False)
```

time: 596 us -> 139 us (0.23)
  the two profiles are of different devices: /device:TPU:2 before, /device:TPU:1 now
where the time goes in v1:
time: 139 us
  Pallas kernels  60.1 us (43%)
  waiting for transfers between devices  43.1 us (31%)
  between operations  13.4 us (10%)
  blocking collectives  11.1 us (8%)
  local copies, waits for them, and re-layouts  7.12 us (5%)
  matrix products  4.26 us (3%)
    pallas_call x1, Pallas kernels, gather_call(): pl.pallas_call(gather_kernel, out_shape=(jax.ShapeDtypeStruct((rows, widt...  34.3 us
    all_gather x1, waiting for transfers between devices, local(): normed = lax.all_gather(normed, 'tp', axis=1, tiled=True)  30.5 us
    pallas_call x1, Pallas kernels, scan_call(): pl.pallas_call(scan_kernel, out_shape=jax.ShapeDtypeStruct((rows, width),...  25.8 us
    all_gather x1, waiting for transfers between devices, local(): whole = lax.all_gather(mine, 'ctx', axis=0, tiled=True)  12.5 us
    all_to_all x1, blocking collectives, local(): mine = lax.all_to_all(mine, 'tp', split_axis=1, concat_axis=0, tiled=True)  11.1 us
    dot_general x1, matrix products, local(): return jnp.dot(normed, whole, preferred_element_type=F32).astype(BF16)  4.26 us
    unnamed x12, local copies, waits for them, and re-layouts  4 us
    transpose x1, local copies, waits for them, and re-layouts, local(): whole.reshape(ctx, tp, share, -1).transpose(1, 0, 2, 3)  3.11 us
  transfers between devices with their start and end apart: 2, of which 2 were waited for; matrix products, arithmetic and copies ran while one was open for 2% of the time, Pallas kernels for 43%

profile of v1, /device:TPU:1, one launch (start us, length us, event | category | flops | bytes accessed | tf_op | source)
XLA Modules:
  0.0 139.1 jit_solution(4837129263774718686)
XLA Ops:
  6.5 0.0 copy-start
  6.5 0.0 all-gather.5.cloned.1.call-start
  6.5 1.6 %copy-done = bf16[256,4096]{1,0:T(8,128)(2,1)S(1)} copy-done((bf16[256,4096]{1,0:T(8,128)(2,1)S(1)}, bf16[256,4096]{1,0:T(8,128)(2,1)}, u32[]{:S(2)}) %copy-start) | copy-done | bytes 2097176
  8.1 11.1 %all_to_all.19 = bf16[8,8,512]{2,0,1:T(8,128)(2,1)} all-to-all(bf16[8,8,512]{2,0,1:T(8,128)(2,1)S(1)} %bitcast.15), channel_id=1, replica_groups=mesh['ctx'=32,'tp'=8] {'tp'}, dimensions={1} | all-to-all | bytes 131072 | tf_op jit(solution)/shard_map/all_to_all | solution.py:371
  19.3 0.0 all-gather.5.cloned.1.call-update
  19.3 0.0 all-gather.3.cloned.1.call-start
  19.3 0.0 copy-start.1
  19.3 1.0 copy-done.1
  20.4 0.0 copy-start.3
  20.4 0.7 copy-done.3
  21.1 0.0 copy-start.5
  21.1 0.7 copy-done.5
  21.8 0.0 copy-start.2
  21.8 0.0 copy-start.4
  21.8 34.3 %gather_maps.1 = (bf16[512,256]{1,0:T(8,128)(2,1)S(1)}, f32[512,256]{1,0:T(8,128)S(1)}, bf16[2,128,256]{2,1,0:T(8,128)(2,1)S(1)}) custom-call(bf16[512,512]{1,0:T(8,128)(2,1)S(1)} %copy-done.1, bf16[3,4096,256]{2,1,0:T(8,128)(2,1)} %wq.1, bf16[2,4096]{1,0:T(2,128)(2,1)S(1)} %bitcast.11, f32[2]{0:T(128)S(1)} %copy-done.5), custom_call_target="tpu_custom_call" | custom-call | tf_op jit(solution)/shard_map/gather_maps/pallas_call | solution.py:312
  56.0 0.0 copy-done.2
  56.0 0.0 copy-done.4
  56.0 25.8 %scan_groups.1 = bf16[512,256]{1,0:T(8,128)(2,1)} custom-call(bf16[512,256]{1,0:T(8,128)(2,1)S(1)} %get-tuple-element.8.p_in, f32[512,256]{1,0:T(8,128)S(1)} %get-tuple-element.9.n_in, bf16[2,128,256]{2,1,0:T(8,128)(2,1)S(1)} %get-tuple-element.10.x_in, f32[2,128,128]{2,1,0:T(8,128)S(1)} %copy-done.2, f32[2,128]{1,0:T(2,128)S(1)} %copy-done.4), custom_call_target="tpu_custom_call" | custom-call | tf_op jit(solution)/shard_map/scan_groups/pallas_call | solution.py:341
  81.9 0.0 all-gather.3.cloned.1.call-update
  81.9 12.5 %all-gather.5.cloned.1.call-done = bf16[2048,512]{1,0:T(8,128)(2,1)} async-done(((bf16[64,512]{1,0:T(8,128)(2,1)}), bf16[2048,512]{1,0:T(8,128)(2,1)}) %all-gather.5.cloned.1.call-update) | async-done | bytes 2097168 | tf_op jit(solution)/shard_map/all_gather | solution.py:372
  94.4 3.1 %copy.8 = bf16[8,32,8,512]{3,2,1,0:T(8,128)(2,1)} copy(bf16[8,32,8,512]{3,2,0,1:T(8,128)(2,1)} %bitcast.12) | data formatting | bytes 4194304 | tf_op jit(solution)/shard_map/transpose | solution.py:373
  97.5 30.5 %all-gather.3.cloned.1.call-done = bf16[512,2048]{1,0:T(8,128)(2,1)} async-done(((bf16[512,256]{1,0:T(8,128)(2,1)}), bf16[512,2048]{1,0:T(8,128)(2,1)}) %all-gather.3.cloned.1.call-update) | async-done | bytes 2097168 | tf_op jit(solution)/shard_map/all_gather | solution.py:376
  128.0 4.3 %convolution_convert_fusion = bf16[512,512]{1,0:T(8,128)(2,1)} fusion(bf16[512,2048]{1,0:T(8,128)(2,1)} %all-gather.3.cloned.1.call-done, bf16[2048,512]{1,0:T(8,128)(2,1)} %bitcast.13), kind=kOutput, calls=%fused_computation | convolution fusion | flops 1074003968 | bytes 4718592 | tf_op jit(solution)/shard_map/dot_general | solution.py:377
  (1 shorter events, 0.0 us)
Async XLA Ops:
  6.5 1.6 %copy-start = (bf16[256,4096]{1,0:T(8,128)(2,1)S(1)}, bf16[256,4096]{1,0:T(8,128)(2,1)}, u32[]{:S(2)}) copy-start(bf16[256,4096]{1,0:T(8,128)(2,1)} %param.13) | copy-start | bytes 6291460
  6.5 87.9 %all-gather.5.cloned.1.call-start = ((), (), s32[]{:S(2)}) async-start(), calls=%async_computation.2 | async-start | bytes 2162688 | tf_op jit(solution)/shard_map/all_gather | solution.py:372
  19.3 108.8 %all-gather.3.cloned.1.call-start = ((), (), s32[]{:S(2)}) async-start(), calls=%async_computation.1 | async-start | bytes 2359296 | tf_op jit(solution)/shard_map/all_gather | solution.py:376
  19.3 1.0 copy-start.1
  20.4 0.7 copy-start.3
  21.1 0.7 copy-start.5
  21.8 34.3 %copy-start.2 = (f32[2,128,128]{2,1,0:T(8,128)S(1)}, f32[2,128,128]{2,1,0:T(8,128)}, u32[]{:S(2)}) copy-start(f32[2,128,128]{2,1,0:T(8,128)} %w0.1) | copy-start | bytes 393220
  21.8 34.3 %copy-start.4 = (f32[2,128]{1,0:T(2,128)S(1)}, f32[2,128]{1,0:T(2,128)}, u32[]{:S(2)}) copy-start(f32[2,128]{1,0:T(2,128)} %gain.1) | copy-start | bytes 3076
Sparse Core Ops, SparseCore 0:
  19.4 74.9 all-gather.4
  96.3 31.7 all-gather.2

commit v2 on v0

v2 whole, which is shorter than its diff:
```python
import jax
import jax.numpy as jnp
from jax import lax
from jax.experimental import pallas as pl
from jax.experimental.pallas import tpu as pltpu
from jax.sharding import PartitionSpec as P

MB = 16
CH = 128
MESH = pl.DeviceIdType.MESH
F32 = jnp.float32
BF16 = jnp.bfloat16
Y, CORES = 4, 2
X, Z = 4, 8
TP = Y * CORES


def dot(a, b):
    return jnp.dot(a.astype(BF16), b.astype(BF16), preferred_element_type=F32)


def compose(later, earlier, hd):
    return earlier + dot(later[:, :hd], earlier) + later


def apply_map(m, w, hd):
    return w + dot(m[:, :hd], w) + m[:, hd:]


def pair_gather(src, buf, width, span, me, send, recv):
    half = span // 2
    sib = me + 1 - 2 * lax.rem(me, 2)
    up, down, far = lax.rem(me + 2, TP), lax.rem(me + TP - 2, TP), lax.rem(me + 4, TP)
    sup, sdown, sfar = lax.rem(sib + 2, TP), lax.rem(sib + TP - 2, TP), lax.rem(sib + 4, TP)
    target = (up, down, sib, up, down, sib, sib, sib, sib)
    leaving = (me, me, me, down, up, down, up, far, far)
    landing = (down, up, sib, far, far, sdown, sup, sfar, sfar)

    def place(ref, kind, c, owner):
        r0 = half if kind in (4, 8) else 0
        n = half if kind in (3, 4, 7, 8) else span
        rs = pl.ds(pl.multiple_of(c * span + r0, 16), n)
        if owner is None:
            return ref.at[rs]
        return ref.at[rs, pl.ds(pl.multiple_of(owner * width, width), width)]

    def out(kind, c):
        own = src is not None and kind < 3
        return pltpu.make_async_remote_copy(
            src_ref=place(src, kind, c, None) if own else place(buf, kind, c, leaving[kind]),
            dst_ref=place(buf, kind, c, leaving[kind]),
            send_sem=send.at[c, kind],
            recv_sem=recv.at[c, kind],
            device_id={"tp": target[kind]},
            device_id_type=MESH,
        )

    def arrived(kind, c):
        ref = place(buf, kind, c, landing[kind])
        pltpu.make_async_remote_copy(
            src_ref=ref, dst_ref=ref, send_sem=send.at[c, kind], recv_sem=recv.at[c, kind],
            device_id={"tp": sib}, device_id_type=MESH,
        ).wait_recv()

    def begin(c):
        out(0, c).start()
        out(1, c).start()

    def share(c):
        out(2, c).start()

    def forward(c):
        arrived(0, c)
        out(3, c).start()
        out(5, c).start()
        arrived(1, c)
        out(4, c).start()
        out(6, c).start()

    def far_forward(c):
        arrived(3, c)
        out(7, c).start()
        arrived(4, c)
        out(8, c).start()

    def sent(c):
        for kind in range(9):
            out(kind, c).wait_send()

    return begin, share, forward, far_forward, arrived, sent


def layer_kernel(hid, wq, lrw, lr, w0, gain, wout, mixed,
                 xg, wbuf, lrt, acc, pref, pbuf, nbuf, xbf, mbuf, tbuf, wst, wob, win, ng, wc,
                 loc, wsem, gsend, grecv, asend, arecv, msend, mrecv, tsend, trecv, osend, orecv, hsend, hrecv):
    rows, feat = hid.shape
    nc = rows // CH
    heads, hd = pref.shape[0], pref.shape[1]
    hs = range(heads)
    width = heads * hd
    ocols = mixed.shape[1]
    me = lax.axis_index("tp")
    ctx = lax.axis_index("ctx")
    core = lax.rem(me, 2)
    chip = me // 2
    z = lax.rem(ctx, Z)
    x = ctx // Z
    base = x * Z

    barrier = pltpu.get_barrier_semaphore()
    for t in range(1, TP):
        pl.semaphore_signal(barrier, inc=1, device_id={"tp": lax.rem(me + t, TP)}, device_id_type=MESH)
    for t in range(1, Z):
        pl.semaphore_signal(barrier, inc=1, device_id={"ctx": base + lax.rem(z + t, Z)}, device_id_type=MESH)
    for t in range(1, X):
        pl.semaphore_signal(barrier, inc=1, device_id={"ctx": lax.rem(ctx + t * Z, X * Z)}, device_id_type=MESH)

    wcopies = [pltpu.make_async_copy(wq.at[c], wbuf.at[:, pl.ds(c * width, width)], wsem.at[c]) for c in range(3)]
    for cp in wcopies:
        cp.start()
    own = pltpu.make_async_copy(hid, xg.at[:, pl.ds(pl.multiple_of(me * feat, feat), feat)], loc.at[0])
    own.start()

    def wout_cols(j):
        return wout.at[:, pl.ds(pl.multiple_of(j * ocols, ocols), ocols)]

    def wc_rows(j):
        return wc.at[pl.ds(pl.multiple_of(j * width, width), width)]

    wown = pltpu.make_async_copy(wout_cols(me), wc_rows(me), loc.at[1])
    wown.start()
    begin, share, forward, far_forward, arrived, sent = pair_gather(hid, xg, feat, CH, me, gsend, grecv)
    pl.semaphore_wait(barrier, TP + Z + X - 3)
    begin(0)
    begin(1)
    for c in range(nc):
        share(c)

    lrt[...] = jnp.zeros_like(lrt)
    lrt[0:heads, :] = lrw[...].astype(F32)

    def gate(i, carry):
        at = pl.ds(pl.multiple_of(i * CH, CH), CH)
        wbuf[at, 3 * width:] = lrt[:, at].T.astype(BF16)
        return carry

    lax.fori_loop(0, wbuf.shape[0] // CH, gate, 0)
    pref[...] = jnp.zeros_like(pref)
    own.wait()
    for cp in wcopies:
        cp.wait()

    def part(c, q):
        rs = pl.ds(pl.multiple_of(c * CH, CH), CH)
        ks = pl.ds(pl.multiple_of(lax.rem(chip + q, Y) * 2 * feat, 2 * feat), 2 * feat)
        return jnp.dot(xg[rs, ks], wbuf[ks, :], preferred_element_type=F32)

    def near(c, carry):
        arrived(2, c)
        acc[pl.ds(pl.multiple_of(c * CH, CH), CH), :] = part(c, 0)
        return carry

    def sides(c):
        arrived(5, c)
        arrived(6, c)
        acc[pl.ds(pl.multiple_of(c * CH, CH), CH), :] += part(c, 1) + part(c, Y - 1)

    lax.fori_loop(0, nc, near, 0)
    forward(0)
    begin(2)
    sides(0)
    forward(1)
    begin(3)
    far_forward(0)
    sides(1)

    row = lax.broadcasted_iota(jnp.int32, (CH, CH), 0)
    col = lax.broadcasted_iota(jnp.int32, (CH, CH), 1)
    causal = row >= col
    before = (row >> 4) > (col >> 4)

    def chunk(c, carry):
        arrived(7, c)
        arrived(8, c)
        rs = pl.ds(pl.multiple_of(c * CH, CH), CH)
        proj = acc[rs, :] + part(c, 2)
        part3 = [[proj[:, (k * heads + h) * hd:(k * heads + h + 1) * hd] for h in hs] for k in range(3)]

        def unit(v):
            return v * lax.rsqrt(jnp.sum(v * v, -1, keepdims=True) + hd * 1e-06)

        q = [unit(part3[0][h]) for h in hs]
        k = [unit(part3[1][h]) for h in hs]
        rate = [lr[h] * jax.nn.sigmoid(proj[:, 3 * width + h:3 * width + h + 1]) for h in hs]
        krt = [(k[h] * rate[h]).T.astype(BF16) for h in hs]
        sg = [dot(jnp.concatenate([q[h], k[h]], 0), krt[h]) for h in hs]
        m = [jnp.where(causal, sg[h][:CH], 0.0).astype(BF16) for h in hs]
        l1 = [jnp.where(before, sg[h][CH:], 0.0) for h in hs]
        lb = [l1[h].astype(BF16) for h in hs]
        l2 = [dot(lb[h], lb[h]) for h in hs]
        l34 = [dot(jnp.concatenate([lb[h], l2[h].astype(BF16)], 0), l2[h]) for h in hs]
        t1 = [l2[h] - l1[h] - l34[h][:CH] for h in hs]
        t = [t1[h] + l34[h][CH:] + dot(t1[h], l34[h][CH:]) for h in hs]
        kv = [jnp.concatenate([k[h], part3[2][h]], 1) for h in hs]
        uy = [kv[h] + dot(t[h], kv[h]) for h in hs]
        dn = [dot(jnp.concatenate([krt[h], m[h]], 0), uy[h]) for h in hs]
        d = [jnp.concatenate([-dn[h][:CH, :hd], dn[h][:CH, hd:]], 1) for h in hs]
        p = [q[h] - dn[h][CH:, :hd] for h in hs]
        n = [dn[h][CH:, hd:] for h in hs]
        x0 = [pref[h] for h in hs]
        dx = [dot(jnp.concatenate([d[h][:, :hd], p[h]], 0), x0[h]) for h in hs]
        for h in hs:
            pref[h] = x0[h] + dx[h][:CH] + d[h]
            pbuf[rs, h * hd:(h + 1) * hd] = (p[h] + dx[h][CH:, :hd]).astype(BF16)
            nbuf[rs, h * hd:(h + 1) * hd] = n[h] + dx[h][CH:, hd:]

        @pl.when(c < nc - 2)
        def _():
            forward(c + 2)

        @pl.when(c < nc - 1)
        def _():
            far_forward(c + 1)

        @pl.when(c < nc - 2)
        def _():
            sides(c + 2)

        return carry

    lax.fori_loop(0, nc, chunk, 0)

    def root(h):
        return 4 * core + 2 * h

    def to_root(h):
        return pltpu.make_async_remote_copy(
            src_ref=xbf.at[h], dst_ref=mbuf.at[z], send_sem=msend.at[h], recv_sem=mrecv.at[z],
            device_id={"ctx": base + root(h)}, device_id_type=MESH,
        )

    for h in hs:
        xbf[h] = pref[h].astype(BF16)

        @pl.when(z != root(h))
        def _():
            to_root(h).start()

        @pl.when(z == root(h))
        def _():
            mbuf[z] = xbf[h]

    def to_column(t):
        j = lax.rem(me + t, TP)
        return pltpu.make_async_remote_copy(
            src_ref=wout_cols(j), dst_ref=wc_rows(me), send_sem=asend.at[t - 1], recv_sem=arecv.at[t - 1],
            device_id={"tp": j}, device_id_type=MESH,
        )

    def from_column(t):
        ref = wc_rows(lax.rem(me + TP - t, TP))
        return pltpu.make_async_remote_copy(
            src_ref=ref, dst_ref=ref, send_sem=asend.at[t - 1], recv_sem=arecv.at[t - 1],
            device_id={"tp": lax.rem(me + t, TP)}, device_id_type=MESH,
        )

    for t in range(1, TP):
        to_column(t).start()

    def to_group(d):
        return pltpu.make_async_remote_copy(
            src_ref=tbuf.at[x], dst_ref=tbuf.at[x], send_sem=tsend.at[d - 1], recv_sem=trecv.at[x],
            device_id={"ctx": lax.rem(ctx + d * Z, X * Z)}, device_id_type=MESH,
        )

    def to_member(h, j):
        return pltpu.make_async_remote_copy(
            src_ref=wob.at[j], dst_ref=win.at[h], send_sem=osend.at[j], recv_sem=orecv.at[h],
            device_id={"ctx": base + j}, device_id_type=MESH,
        )

    is_root = (z == root(0)) | (z == root(1))
    mine = lax.rem(z, 4) // 2

    @pl.when(is_root)
    def _():
        for j in range(Z):
            @pl.when(z != j)
            def _():
                pltpu.make_async_remote_copy(
                    src_ref=mbuf.at[j], dst_ref=mbuf.at[j], send_sem=msend.at[0], recv_sem=mrecv.at[j],
                    device_id={"ctx": base + lax.rem(z + 1, Z)}, device_id_type=MESH,
                ).wait_recv()
        ms = [mbuf[j].astype(F32) for j in range(Z)]
        pr = [compose(ms[2 * j + 1], ms[2 * j], hd) for j in range(Z // 2)]
        qd = [compose(pr[2 * j + 1], pr[2 * j], hd) for j in range(Z // 4)]
        tbuf[x] = compose(qd[1], qd[0], hd).astype(BF16)
        for d in range(1, X):
            @pl.when(x + d < X)
            def _():
                to_group(d).start()
        six = compose(pr[2], qd[0], hd)
        pre = [None, ms[0], pr[0], compose(ms[2], pr[0], hd), qd[0], compose(ms[4], qd[0], hd), six,
               compose(ms[6], six, hd)]
        wst[...] = w0[mine]
        for j in range(X - 1):
            @pl.when(j < x)
            def _():
                pltpu.make_async_remote_copy(
                    src_ref=tbuf.at[j], dst_ref=tbuf.at[j], send_sem=tsend.at[0], recv_sem=trecv.at[j],
                    device_id={"ctx": lax.rem(ctx + Z, X * Z)}, device_id_type=MESH,
                ).wait_recv()
                wst[...] = apply_map(tbuf[j].astype(F32), wst[...], hd)
        w = wst[...]
        for j in range(Z):
            wob[j] = (w if j == 0 else apply_map(pre[j], w, hd)).astype(BF16)
        for j in range(Z):
            @pl.when(z != j)
            def _():
                to_member(mine, j).start()
        win[mine] = wob[z]

    gbegin, gshare, gforward, gfar_forward, garrived, gsent = pair_gather(
        None, ng, width, rows // 2, me, hsend, hrecv)
    for h in hs:
        @pl.when(z != root(h))
        def _():
            pltpu.make_async_remote_copy(
                src_ref=win.at[h], dst_ref=win.at[h], send_sem=osend.at[0], recv_sem=orecv.at[h],
                device_id={"ctx": base + lax.rem(z + 1, Z)}, device_id_type=MESH,
            ).wait_recv()
    for c in range(2):
        rs = slice(c * (rows // 2), (c + 1) * (rows // 2))
        for h in hs:
            hc = slice(h * hd, (h + 1) * hd)
            zv = dot(pbuf[rs, hc], win[h]) + nbuf[rs, hc]
            zv = zv * lax.rsqrt(jnp.mean(zv * zv, -1, keepdims=True) + 1e-06) * gain[h:h + 1, :]
            ng[rs, pl.ds(pl.multiple_of(me * width + h * hd, hd), hd)] = zv.astype(BF16)
        gbegin(c)
        gshare(c)
    for c in range(2):
        gforward(c)
    for t in range(1, TP):
        from_column(t).wait_recv()
    wown.wait()
    for c in range(2):
        gfar_forward(c)
    for c in range(2):
        for kind in (2, 5, 6, 7, 8):
            garrived(kind, c)
        rs = slice(c * (rows // 2), (c + 1) * (rows // 2))
        mixed[rs, :] = jnp.dot(ng[rs, :], wc[...], preferred_element_type=F32).astype(BF16)

    def drain(c, carry):
        sent(c)
        return carry

    lax.fori_loop(0, nc, drain, 0)
    for c in range(2):
        gsent(c)
    for t in range(1, TP):
        to_column(t).wait_send()
    for h in hs:
        @pl.when(z != root(h))
        def _():
            to_root(h).wait_send()

    @pl.when(is_root)
    def _():
        for d in range(1, X):
            @pl.when(x + d < X)
            def _():
                to_group(d).wait_send()
        for j in range(Z):
            @pl.when(z != j)
            def _():
                to_member(mine, j).wait_send()


def any_spec():
    return pl.BlockSpec(memory_space=pl.ANY)


def vmem_spec():
    return pl.BlockSpec(memory_space=pltpu.VMEM)


def local(hidden_in, w_qkv, lr_weight, inner_lr, init_state, norm_gain, w_out):
    rows, feat = hidden_in.shape
    _, depth, width = w_qkv.shape
    heads, hd = norm_gain.shape
    nc = rows // CH
    out_cols = w_out.shape[1] // TP
    dma = pltpu.SemaphoreType.DMA
    return pl.pallas_call(
        layer_kernel,
        out_shape=jax.ShapeDtypeStruct((rows, out_cols), BF16),
        in_specs=[any_spec(), any_spec(), vmem_spec(), pl.BlockSpec(memory_space=pltpu.SMEM),
                  vmem_spec(), vmem_spec(), any_spec()],
        out_specs=vmem_spec(),
        scratch_shapes=[
            pltpu.VMEM((rows, depth), BF16),
            pltpu.VMEM((depth, 3 * width + CH), BF16),
            pltpu.VMEM((CH, depth), F32),
            pltpu.VMEM((rows, 3 * width + CH), F32),
            pltpu.VMEM((heads, hd, 2 * hd), F32),
            pltpu.VMEM((rows, width), BF16),
            pltpu.VMEM((rows, width), F32),
            pltpu.VMEM((heads, hd, 2 * hd), BF16),
            pltpu.VMEM((Z, hd, 2 * hd), BF16),
            pltpu.VMEM((X, hd, 2 * hd), BF16),
            pltpu.VMEM((hd, hd), F32),
            pltpu.VMEM((Z, hd, hd), BF16),
            pltpu.VMEM((heads, hd, hd), BF16),
            pltpu.VMEM((rows, TP * width), BF16),
            pltpu.VMEM((TP * width, out_cols), BF16),
            dma((2,)),
            dma((3,)),
            dma((nc, 9)),
            dma((nc, 9)),
            dma((TP - 1,)),
            dma((TP - 1,)),
            dma((heads,)),
            dma((Z,)),
            dma((X - 1,)),
            dma((X,)),
            dma((Z,)),
            dma((heads,)),
            dma((2, 9)),
            dma((2, 9)),
        ],
        compiler_params=pltpu.CompilerParams(
            collective_id=0, has_side_effects=True, vmem_limit_bytes=48 * 1024 * 1024
        ),
        name="layer",
    )(hidden_in, w_qkv, lr_weight.T, inner_lr, init_state, norm_gain, w_out)


def solution(mesh):
    in_specs = (
        P("ctx", "tp"),
        P(None, None, "tp"),
        P(None, "tp"),
        P("tp"),
        P("tp", None, None),
        P("tp", None),
        P("tp", None),
    )
    out_specs = P("ctx", "tp")
    return jax.shard_map(local, mesh=mesh, in_specs=in_specs, out_specs=out_specs, check_vma=False)
```

time: 596 us -> 77.8 us (0.13)
  the two profiles are of different devices: /device:TPU:2 before, /device:TPU:1 now
where the time goes in v2:
time: 77.8 us; the launch traced here: 77.5 us
  Pallas kernels  71.1 us (91%)
  local copies, waits for them, and re-layouts  6.38 us (8%)
    pallas_call x1, Pallas kernels, local(): pl.pallas_call(layer_kernel, out_shape=jax.ShapeDtypeStruct((rows, out_co...  71.1 us
    unnamed x13, local copies, waits for them, and re-layouts  6.38 us

profile of v2, /device:TPU:1, one launch (start us, length us, event | category | flops | bytes accessed | tf_op | source)
XLA Modules:
  0.0 77.5 jit_solution(4449933259309097781)
XLA Ops:
  0.0 0.0 copy-start
  0.0 1.6 %copy-done = bf16[256,4096]{1,0:T(8,128)(2,1)S(1)} copy-done((bf16[256,4096]{1,0:T(8,128)(2,1)S(1)}, bf16[256,4096]{1,0:T(8,128)(2,1)}, u32[]{:S(2)}) %copy-start) | copy-done | bytes 2097176
  1.6 0.0 copy-start.1
  1.6 1.0 %copy-done.1 = bf16[512,512]{1,0:T(8,128)(2,1)S(1)} copy-done((bf16[512,512]{1,0:T(8,128)(2,1)S(1)}, bf16[512,512]{1,0:T(8,128)(2,1)}, u32[]{:S(2)}) %copy-start.1) | copy-done | bytes 524312
  2.6 0.0 copy-start.2
  2.6 0.9 %copy-done.2 = f32[2,128,128]{2,1,0:T(8,128)S(1)} copy-done((f32[2,128,128]{2,1,0:T(8,128)S(1)}, f32[2,128,128]{2,1,0:T(8,128)}, u32[]{:S(2)}) %copy-start.2) | copy-done | bytes 131096
  3.5 0.0 copy-start.3
  3.5 0.7 copy-done.3
  4.3 0.0 copy-start.4
  4.3 0.7 copy-done.4
  4.9 0.0 copy-start.5
  4.9 0.7 copy-done.5
  5.6 71.1 %layer.1 = bf16[512,512]{1,0:T(8,128)(2,1)S(1)} custom-call(bf16[512,512]{1,0:T(8,128)(2,1)S(1)} %copy-done.1, bf16[3,4096,256]{2,1,0:T(8,128)(2,1)} %wq.1, bf16[2,4096]{1,0:T(2,128)(2,1)S(1)} %bitcast.1, f32[2]{0:T(128)S(1)} %copy-done.5, f32[2,128,128]{2,1,0:T(8,128)S(1)} %copy-done.2, f32[2,128]{1,0:T(2,128)S(1)} %copy-done.4, bf16[256,4096]{1,0:T(8,128)(2,1)S(1)} %copy-done), custom_call_target="tpu_custom_call" | custom-call | tf_op jit(solution)/shard_map/layer/pallas_call | solution.py:395
  76.7 0.8 %copy.9 = bf16[512,512]{1,0:T(8,128)(2,1)} copy(bf16[512,512]{1,0:T(8,128)(2,1)S(1)} %layer.1) | data formatting | bytes 1048576
Async XLA Ops:
  0.0 1.6 %copy-start = (bf16[256,4096]{1,0:T(8,128)(2,1)S(1)}, bf16[256,4096]{1,0:T(8,128)(2,1)}, u32[]{:S(2)}) copy-start(bf16[256,4096]{1,0:T(8,128)(2,1)} %wout.1) | copy-start | bytes 6291460
  1.6 1.0 %copy-start.1 = (bf16[512,512]{1,0:T(8,128)(2,1)S(1)}, bf16[512,512]{1,0:T(8,128)(2,1)}, u32[]{:S(2)}) copy-start(bf16[512,512]{1,0:T(8,128)(2,1)} %hid.1) | copy-start | bytes 1572868
  2.6 0.9 %copy-start.2 = (f32[2,128,128]{2,1,0:T(8,128)S(1)}, f32[2,128,128]{2,1,0:T(8,128)}, u32[]{:S(2)}) copy-start(f32[2,128,128]{2,1,0:T(8,128)} %w0.1) | copy-start | bytes 393220
  3.5 0.7 copy-start.3
  4.3 0.7 copy-start.4
  4.9 0.7 copy-start.5

commit v3 on v2

--- a/solution.py
+++ b/solution.py
@@ -90,9 +90,9 @@
     return begin, share, forward, far_forward, arrived, sent
 
 
-def layer_kernel(hid, wq, lrw, lr, w0, gain, wout, mixed,
-                 xg, wbuf, lrt, acc, pref, pbuf, nbuf, xbf, mbuf, tbuf, wst, wob, win, ng, wc,
-                 loc, wsem, gsend, grecv, asend, arecv, msend, mrecv, tsend, trecv, osend, orecv, hsend, hrecv):
+def layer_kernel(hid, wq, lrw_in, lr_in, w0_in, gain_in, wout, mixed,
+                 lrw, lr, w0, gain, xg, wbuf, lrt, acc, pref, pbuf, nbuf, xbf, mbuf, tbuf, wst, wob, win, ng, wc,
+                 loc, lsem, wsem, gsend, grecv, asend, arecv, msend, mrecv, tsend, trecv, osend, orecv, hsend, hrecv):
     rows, feat = hid.shape
     nc = rows // CH
     heads, hd = pref.shape[0], pref.shape[1]
@@ -107,6 +107,12 @@
     x = ctx // Z
     base = x * Z
 
+    smalls = [
+        pltpu.make_async_copy(a, b, lsem.at[i])
+        for i, (a, b) in enumerate(((lrw_in, lrw), (lr_in, lr), (w0_in, w0), (gain_in, gain)))
+    ]
+    for cp in smalls:
+        cp.start()
     barrier = pltpu.get_barrier_semaphore()
     for t in range(1, TP):
         pl.semaphore_signal(barrier, inc=1, device_id={"tp": lax.rem(me + t, TP)}, device_id_type=MESH)
@@ -137,6 +143,8 @@
         share(c)
 
     lrt[...] = jnp.zeros_like(lrt)
+    for cp in smalls:
+        cp.wait()
     lrt[0:heads, :] = lrw[...].astype(F32)
 
     def gate(i, carry):
@@ -149,6 +157,20 @@
     own.wait()
     for cp in wcopies:
         cp.wait()
+
+    def to_column(t):
+        j = lax.rem(me + t, TP)
+        return pltpu.make_async_remote_copy(
+            src_ref=wout_cols(j), dst_ref=wc_rows(me), send_sem=asend.at[t - 1], recv_sem=arecv.at[t - 1],
+            device_id={"tp": j}, device_id_type=MESH,
+        )
+
+    def from_column(t):
+        ref = wc_rows(lax.rem(me + TP - t, TP))
+        return pltpu.make_async_remote_copy(
+            src_ref=ref, dst_ref=ref, send_sem=asend.at[t - 1], recv_sem=arecv.at[t - 1],
+            device_id={"tp": lax.rem(me + t, TP)}, device_id_type=MESH,
+        )
 
     def part(c, q):
         rs = pl.ds(pl.multiple_of(c * CH, CH), CH)
@@ -222,6 +244,11 @@
         def _():
             far_forward(c + 1)
 
+        @pl.when(c == nc - 2)
+        def _():
+            for t in range(1, TP):
+                to_column(t).start()
+
         @pl.when(c < nc - 2)
         def _():
             sides(c + 2)
@@ -249,23 +276,6 @@
         @pl.when(z == root(h))
         def _():
             mbuf[z] = xbf[h]
-
-    def to_column(t):
-        j = lax.rem(me + t, TP)
-        return pltpu.make_async_remote_copy(
-            src_ref=wout_cols(j), dst_ref=wc_rows(me), send_sem=asend.at[t - 1], recv_sem=arecv.at[t - 1],
-            device_id={"tp": j}, device_id_type=MESH,
-        )
-
-    def from_column(t):
-        ref = wc_rows(lax.rem(me + TP - t, TP))
-        return pltpu.make_async_remote_copy(
-            src_ref=ref, dst_ref=ref, send_sem=asend.at[t - 1], recv_sem=arecv.at[t - 1],
-            device_id={"tp": lax.rem(me + t, TP)}, device_id_type=MESH,
-        )
-
-    for t in range(1, TP):
-        to_column(t).start()
 
     def to_group(d):
         return pltpu.make_async_remote_copy(
@@ -377,10 +387,6 @@
                 to_member(mine, j).wait_send()
 
 
-def any_spec():
-    return pl.BlockSpec(memory_space=pl.ANY)
-
-
 def vmem_spec():
     return pl.BlockSpec(memory_space=pltpu.VMEM)
 
@@ -395,10 +401,13 @@
     return pl.pallas_call(
         layer_kernel,
         out_shape=jax.ShapeDtypeStruct((rows, out_cols), BF16),
-        in_specs=[any_spec(), any_spec(), vmem_spec(), pl.BlockSpec(memory_space=pltpu.SMEM),
-                  vmem_spec(), vmem_spec(), any_spec()],
+        in_specs=[pl.BlockSpec(memory_space=pltpu.HBM)] * 7,
         out_specs=vmem_spec(),
         scratch_shapes=[
+            pltpu.VMEM((heads, depth), BF16),
+            pltpu.SMEM((heads,), F32),
+            pltpu.VMEM((heads, hd, hd), F32),
+            pltpu.VMEM((heads, hd), F32),
             pltpu.VMEM((rows, depth), BF16),
             pltpu.VMEM((depth, 3 * width + CH), BF16),
             pltpu.VMEM((CH, depth), F32),
@@ -415,6 +424,7 @@
             pltpu.VMEM((rows, TP * width), BF16),
             pltpu.VMEM((TP * width, out_cols), BF16),
             dma((2,)),
+            dma((4,)),
             dma((3,)),
             dma((nc, 9)),
             dma((nc, 9)),

time: 77.8 us -> 74.4 us (0.956)
  Pallas kernels: 71.1 us -> 67.7 us
    pallas_call x1, Pallas kernels: 71.1 us -> 67.7 us  [local(): pl.pallas_call(layer_kernel, out_shape=jax.ShapeDtypeStruct((rows, out_co...]
where the time goes in v3:
time: 74.4 us; the launch traced here: 74.1 us
  Pallas kernels  67.7 us (91%)
  local copies, waits for them, and re-layouts  6.38 us (9%)
    pallas_call x1, Pallas kernels, local(): pl.pallas_call(layer_kernel, out_shape=jax.ShapeDtypeStruct((rows, out_co...  67.7 us
    unnamed x13, local copies, waits for them, and re-layouts  6.38 us

profile of v3, /device:TPU:1, one launch (start us, length us, event | category | flops | bytes accessed | tf_op | source)
XLA Modules:
  0.0 74.1 jit_solution(846586015678481518)
XLA Ops:
  0.0 0.0 copy-start
  0.0 1.6 %copy-done = bf16[256,4096]{1,0:T(8,128)(2,1)S(1)} copy-done((bf16[256,4096]{1,0:T(8,128)(2,1)S(1)}, bf16[256,4096]{1,0:T(8,128)(2,1)}, u32[]{:S(2)}) %copy-start) | copy-done | bytes 2097176
  1.6 0.0 copy-start.1
  1.6 1.0 %copy-done.1 = bf16[512,512]{1,0:T(8,128)(2,1)S(1)} copy-done((bf16[512,512]{1,0:T(8,128)(2,1)S(1)}, bf16[512,512]{1,0:T(8,128)(2,1)}, u32[]{:S(2)}) %copy-start.1) | copy-done | bytes 524312
  2.6 0.0 copy-start.2
  2.6 0.9 %copy-done.2 = f32[2,128,128]{2,1,0:T(8,128)S(1)} copy-done((f32[2,128,128]{2,1,0:T(8,128)S(1)}, f32[2,128,128]{2,1,0:T(8,128)}, u32[]{:S(2)}) %copy-start.2) | copy-done | bytes 131096
  3.5 0.0 copy-start.3
  3.5 0.7 copy-done.3
  4.3 0.0 copy-start.4
  4.3 0.7 copy-done.4
  4.9 0.0 copy-start.5
  4.9 0.7 copy-done.5
  5.6 67.7 %layer.1 = bf16[512,512]{1,0:T(8,128)(2,1)S(1)} custom-call(bf16[512,512]{1,0:T(8,128)(2,1)S(1)} %copy-done.1, bf16[3,4096,256]{2,1,0:T(8,128)(2,1)} %wq.1, bf16[2,4096]{1,0:T(2,128)(2,1)S(1)} %bitcast.1, f32[2]{0:T(128)S(1)} %copy-done.5, f32[2,128,128]{2,1,0:T(8,128)S(1)} %copy-done.2, f32[2,128]{1,0:T(2,128)S(1)} %copy-done.4, bf16[256,4096]{1,0:T(8,128)(2,1)S(1)} %copy-done), custom_call_target="tpu_custom_call" | custom-call | tf_op jit(solution)/shard_map/layer/pallas_call | solution.py:401
  73.3 0.8 %copy.9 = bf16[512,512]{1,0:T(8,128)(2,1)} copy(bf16[512,512]{1,0:T(8,128)(2,1)S(1)} %layer.1) | data formatting | bytes 1048576
Async XLA Ops:
  0.0 1.6 %copy-start = (bf16[256,4096]{1,0:T(8,128)(2,1)S(1)}, bf16[256,4096]{1,0:T(8,128)(2,1)}, u32[]{:S(2)}) copy-start(bf16[256,4096]{1,0:T(8,128)(2,1)} %wout.1) | copy-start | bytes 6291460
  1.6 1.0 %copy-start.1 = (bf16[512,512]{1,0:T(8,128)(2,1)S(1)}, bf16[512,512]{1,0:T(8,128)(2,1)}, u32[]{:S(2)}) copy-start(bf16[512,512]{1,0:T(8,128)(2,1)} %hid.1) | copy-start | bytes 1572868
  2.6 0.9 %copy-start.2 = (f32[2,128,128]{2,1,0:T(8,128)S(1)}, f32[2,128,128]{2,1,0:T(8,128)}, u32[]{:S(2)}) copy-start(f32[2,128,128]{2,1,0:T(8,128)} %w0_in.1) | copy-start | bytes 393220
  3.5 0.7 copy-start.3
  4.3 0.7 copy-start.4
  4.9 0.7 copy-start.5

commit v4 on v3

--- a/solution.py
+++ b/solution.py
@@ -398,6 +398,8 @@
     nc = rows // CH
     out_cols = w_out.shape[1] // TP
     dma = pltpu.SemaphoreType.DMA
+    operands = (hidden_in, w_qkv, lr_weight.T, inner_lr, init_state, norm_gain, w_out)
+    operands = [pltpu.with_memory_space_constraint(a, pltpu.HBM) for a in operands]
     return pl.pallas_call(
         layer_kernel,
         out_shape=jax.ShapeDtypeStruct((rows, out_cols), BF16),
@@ -443,7 +445,7 @@
             collective_id=0, has_side_effects=True, vmem_limit_bytes=48 * 1024 * 1024
         ),
         name="layer",
-    )(hidden_in, w_qkv, lr_weight.T, inner_lr, init_state, norm_gain, w_out)
+    )(*operands)
 
 
 def solution(mesh):

time: 74.4 us -> 68.7 us (0.923)
  local copies, waits for them, and re-layouts: 6.38 us -> 0.8 us
    unnamed x13 -> x1, local copies, waits for them, and re-layouts: 6.38 us -> 0.8 us
where the time goes in v4:
time: 68.7 us; the launch traced here: 68.6 us
  Pallas kernels  67.8 us (99%)
  local copies, waits for them, and re-layouts  0.8 us (1%)
    pallas_call x1, Pallas kernels, local(): pl.pallas_call(layer_kernel, out_shape=jax.ShapeDtypeStruct((rows, out_co...  67.8 us

profile of v4, /device:TPU:1, one launch (start us, length us, event | category | flops | bytes accessed | tf_op | source)
XLA Modules:
  0.0 68.6 jit_solution(16851848951157542191)
XLA Ops:
  0.0 67.8 %layer.1 = bf16[512,512]{1,0:T(8,128)(2,1)S(1)} custom-call(bf16[512,512]{1,0:T(8,128)(2,1)} %hid.1, bf16[3,4096,256]{2,1,0:T(8,128)(2,1)} %wq.1, bf16[2,4096]{1,0:T(2,128)(2,1)} %bitcast.1, f32[2]{0:T(128)} %lr_in.1, f32[2,128,128]{2,1,0:T(8,128)} %w0_in.1, f32[2,128]{1,0:T(2,128)} %gain_in.1, bf16[256,4096]{1,0:T(8,128)(2,1)} %wout.1), custom_call_target="tpu_custom_call" | custom-call | tf_op jit(solution)/shard_map/layer/pallas_call | solution.py:403
  67.9 0.8 %copy.9 = bf16[512,512]{1,0:T(8,128)(2,1)} copy(bf16[512,512]{1,0:T(8,128)(2,1)S(1)} %layer.1) | data formatting | bytes 1048576

commit v5 on v4

--- a/solution.py
+++ b/solution.py
@@ -27,7 +27,7 @@
     return w + dot(m[:, :hd], w) + m[:, hd:]
 
 
-def pair_gather(src, buf, width, span, me, send, recv):
+def pair_gather(src, buf, span, me, send, recv):
     half = span // 2
     sib = me + 1 - 2 * lax.rem(me, 2)
     up, down, far = lax.rem(me + 2, TP), lax.rem(me + TP - 2, TP), lax.rem(me + 4, TP)
@@ -40,9 +40,7 @@
         r0 = half if kind in (4, 8) else 0
         n = half if kind in (3, 4, 7, 8) else span
         rs = pl.ds(pl.multiple_of(c * span + r0, 16), n)
-        if owner is None:
-            return ref.at[rs]
-        return ref.at[rs, pl.ds(pl.multiple_of(owner * width, width), width)]
+        return ref.at[rs] if owner is None else ref.at[owner, rs]
 
     def out(kind, c):
         own = src is not None and kind < 3
@@ -91,8 +89,9 @@
 
 
 def layer_kernel(hid, wq, lrw_in, lr_in, w0_in, gain_in, wout, mixed,
-                 lrw, lr, w0, gain, xg, wbuf, lrt, acc, pref, pbuf, nbuf, xbf, mbuf, tbuf, wst, wob, win, ng, wc,
-                 loc, lsem, wsem, gsend, grecv, asend, arecv, msend, mrecv, tsend, trecv, osend, orecv, hsend, hrecv):
+                 lrw, lr, w0, gain, gall, xg, wbuf, wgate, lrt, acc, pref, xbf, mbuf, tbuf, pre, wst, wob, pn, wg, abuf, bbuf, total,
+                 loc, lsem, wsem, gsend, grecv, psend, precv, hsend, hrecv, msend, mrecv, tsend, trecv, osend, orecv,
+                 ysend, yrecv, axsend, axrecv, azsend, azrecv, bzsend, bzrecv, bxsend, bxrecv):
     rows, feat = hid.shape
     nc = rows // CH
     heads, hd = pref.shape[0], pref.shape[1]
@@ -121,61 +120,153 @@
     for t in range(1, X):
         pl.semaphore_signal(barrier, inc=1, device_id={"ctx": lax.rem(ctx + t * Z, X * Z)}, device_id_type=MESH)
 
-    wcopies = [pltpu.make_async_copy(wq.at[c], wbuf.at[:, pl.ds(c * width, width)], wsem.at[c]) for c in range(3)]
+    wcopies = [pltpu.make_async_copy(wq.at[c], wbuf.at[c], wsem.at[c]) for c in range(3)]
     for cp in wcopies:
         cp.start()
-    own = pltpu.make_async_copy(hid, xg.at[:, pl.ds(pl.multiple_of(me * feat, feat), feat)], loc.at[0])
+    own = pltpu.make_async_copy(hid, xg.at[me], loc.at[0])
     own.start()
 
-    def wout_cols(j):
-        return wout.at[:, pl.ds(pl.multiple_of(j * ocols, ocols), ocols)]
-
-    def wc_rows(j):
-        return wc.at[pl.ds(pl.multiple_of(j * width, width), width)]
-
-    wown = pltpu.make_async_copy(wout_cols(me), wc_rows(me), loc.at[1])
-    wown.start()
-    begin, share, forward, far_forward, arrived, sent = pair_gather(hid, xg, feat, CH, me, gsend, grecv)
+    bblock = 8 + 2 * x + z // 4
+    blocks = ((z, x), (bblock, lax.rem(z, 4)))
+
+    def piece_in(kind, j):
+        block, cb = blocks[kind]
+        at = pl.multiple_of(j * ocols + cb * CH, CH)
+        return wout.at[pl.ds(pl.multiple_of(block * MB, MB), MB), pl.ds(at, CH)]
+
+    def piece(kind, j):
+        return abuf.at[z, x, j] if kind == 0 else bbuf.at[x, z, j]
+
+    def pieces(kind, cx, cz):
+        return abuf.at[cz, cx] if kind == 0 else bbuf.at[cx, cz]
+
+    def remote(src, dst, ss, rr, to):
+        return pltpu.make_async_remote_copy(
+            src_ref=src, dst_ref=dst, send_sem=ss, recv_sem=rr, device_id=to, device_id_type=MESH)
+
+    def landed(ref, rr):
+        remote(ref, ref, loc.at[0], rr, {"tp": lax.rem(me + 1, TP)}).wait_recv()
+
+    def on_tp(t):
+        return {"tp": lax.rem(me + t, TP)}
+
+    def on_z(t):
+        return {"ctx": base + lax.rem(z + t, Z)}
+
+    def on_x(t):
+        return {"ctx": lax.rem(ctx + t * Z, X * Z)}
+
+    def y_copy(kind, t):
+        return remote(piece_in(kind, lax.rem(me + t, TP)), piece(kind, me), ysend.at[kind, t - 1],
+                      yrecv.at[kind, t - 1], on_tp(t))
+
+    def gain_copy(t):
+        return remote(gall.at[me], gall.at[me], ysend.at[2, t - 1], yrecv.at[2, t - 1], on_tp(t))
+
+    def ax_copy(t):
+        ref = pieces(0, x, z)
+        return remote(ref, ref, axsend.at[t - 1], axrecv.at[t - 1], on_x(t))
+
+    def bz_copy(t):
+        ref = pieces(1, x, z)
+        return remote(ref, ref, bzsend.at[t - 1], bzrecv.at[t - 1], on_z(t))
+
+    def b_rows(cx):
+        return bbuf.at[cx]
+
+    def bx_copy(t):
+        return remote(b_rows(x), b_rows(x), bxsend.at[t - 1], bxrecv.at[t - 1], on_x(t))
+
+    az_hops = (1, 2, Z - 1, Z - 2, 1, Z - 1, 2, Z - 2)
+    az_from = (0, 0, 0, 0, Z - 2, 2, Z - 2, 2)
+
+    def az_ref(k, block):
+        block = lax.rem(block + 2 * Z, Z)
+        if k < 6:
+            return abuf.at[block]
+        return abuf.at[block, pl.ds((k - 6) * (X // 2), X // 2)]
+
+    def az_copy(k):
+        ref = az_ref(k, z + az_from[k])
+        return remote(ref, ref, azsend.at[k], azrecv.at[k], on_z(az_hops[k]))
+
+    def az_landed(k):
+        landed(az_ref(k, z + az_from[k] - az_hops[k]), azrecv.at[k])
+
+    def az_near():
+        for k in (1, 3, 0, 2):
+            az_copy(k).start()
+
+    def az_far():
+        az_landed(1)
+        az_landed(3)
+        for k in range(4, 8):
+            az_copy(k).start()
+
+    def spread_first():
+        for t in range(1, TP):
+            j = lax.rem(me + TP - t, TP)
+            landed(piece(0, j), yrecv.at[0, t - 1])
+            landed(piece(1, j), yrecv.at[1, t - 1])
+        for cp in wown:
+            cp.wait()
+        for t in range(1, X):
+            ax_copy(t).start()
+        for t in range(1, Z):
+            bz_copy(t).start()
+
+    def spread_z():
+        for t in range(1, X):
+            landed(pieces(0, lax.rem(x + X - t, X), z), axrecv.at[t - 1])
+        az_near()
+
+    def spread_x():
+        for t in range(1, Z):
+            landed(pieces(1, x, lax.rem(z + Z - t, Z)), bzrecv.at[t - 1])
+        for t in range(1, X):
+            bx_copy(t).start()
+
+    wown = [pltpu.make_async_copy(piece_in(kind, me), piece(kind, me), loc.at[1 + kind]) for kind in range(2)]
+    for cp in wown:
+        cp.start()
+    begin, share, forward, far_forward, arrived, sent = pair_gather(hid, xg, CH, me, gsend, grecv)
+    pbegin, pshare, pforward, pfar_forward, parrived, psent = pair_gather(None, pn, CH, me, psend, precv)
     pl.semaphore_wait(barrier, TP + Z + X - 3)
     begin(0)
     begin(1)
     for c in range(nc):
         share(c)
+    for t in range(1, TP):
+        y_copy(0, t).start()
+        y_copy(1, t).start()
 
     lrt[...] = jnp.zeros_like(lrt)
     for cp in smalls:
         cp.wait()
+    gall[me] = jnp.zeros_like(gall[me])
+    gall[me, 0:heads, :] = gain[...]
+    for t in range(1, TP):
+        gain_copy(t).start()
     lrt[0:heads, :] = lrw[...].astype(F32)
 
     def gate(i, carry):
         at = pl.ds(pl.multiple_of(i * CH, CH), CH)
-        wbuf[at, 3 * width:] = lrt[:, at].T.astype(BF16)
+        wgate[at, :] = lrt[:, at].T.astype(BF16)
         return carry
 
-    lax.fori_loop(0, wbuf.shape[0] // CH, gate, 0)
+    lax.fori_loop(0, wgate.shape[0] // CH, gate, 0)
     pref[...] = jnp.zeros_like(pref)
     own.wait()
     for cp in wcopies:
         cp.wait()
 
-    def to_column(t):
-        j = lax.rem(me + t, TP)
-        return pltpu.make_async_remote_copy(
-            src_ref=wout_cols(j), dst_ref=wc_rows(me), send_sem=asend.at[t - 1], recv_sem=arecv.at[t - 1],
-            device_id={"tp": j}, device_id_type=MESH,
-        )
-
-    def from_column(t):
-        ref = wc_rows(lax.rem(me + TP - t, TP))
-        return pltpu.make_async_remote_copy(
-            src_ref=ref, dst_ref=ref, send_sem=asend.at[t - 1], recv_sem=arecv.at[t - 1],
-            device_id={"tp": lax.rem(me + t, TP)}, device_id_type=MESH,
-        )
-
     def part(c, q):
         rs = pl.ds(pl.multiple_of(c * CH, CH), CH)
-        ks = pl.ds(pl.multiple_of(lax.rem(chip + q, Y) * 2 * feat, 2 * feat), 2 * feat)
-        return jnp.dot(xg[rs, ks], wbuf[ks, :], preferred_element_type=F32)
+        cj = lax.rem(chip + q, Y)
+        ks = pl.ds(pl.multiple_of(cj * 2 * feat, 2 * feat), 2 * feat)
+        xs = jnp.concatenate([xg[2 * cj, rs], xg[2 * cj + 1, rs]], 1)
+        weights = [wbuf[i, ks, :] for i in range(3)] + [wgate[ks, :]]
+        return jnp.concatenate([jnp.dot(xs, w, preferred_element_type=F32) for w in weights], 1)
 
     def near(c, carry):
         arrived(2, c)
@@ -190,6 +281,7 @@
     lax.fori_loop(0, nc, near, 0)
     forward(0)
     begin(2)
+    spread_first()
     sides(0)
     forward(1)
     begin(3)
@@ -233,8 +325,8 @@
         dx = [dot(jnp.concatenate([d[h][:, :hd], p[h]], 0), x0[h]) for h in hs]
         for h in hs:
             pref[h] = x0[h] + dx[h][:CH] + d[h]
-            pbuf[rs, h * hd:(h + 1) * hd] = (p[h] + dx[h][CH:, :hd]).astype(BF16)
-            nbuf[rs, h * hd:(h + 1) * hd] = n[h] + dx[h][CH:, hd:]
+            pn[me, rs, h * hd:(h + 1) * hd] = (p[h] + dx[h][CH:, :hd]).astype(BF16)
+            pn[me, rs, width + h * hd:width + (h + 1) * hd] = (n[h] + dx[h][CH:, hd:]).astype(BF16)
 
         @pl.when(c < nc - 2)
         def _():
@@ -246,12 +338,21 @@
 
         @pl.when(c == nc - 2)
         def _():
-            for t in range(1, TP):
-                to_column(t).start()
+            for k in range(nc - 1):
+                pbegin(k)
+                pshare(k)
 
         @pl.when(c < nc - 2)
         def _():
             sides(c + 2)
+
+        @pl.when(c == 0)
+        def _():
+            spread_z()
+
+        @pl.when(c == 1)
+        def _():
+            spread_x()
 
         return carry
 
@@ -277,17 +378,20 @@
         def _():
             mbuf[z] = xbf[h]
 
+    pbegin(nc - 1)
+    pshare(nc - 1)
+    pforward(0)
+    az_far()
+    pforward(1)
+
     def to_group(d):
-        return pltpu.make_async_remote_copy(
-            src_ref=tbuf.at[x], dst_ref=tbuf.at[x], send_sem=tsend.at[d - 1], recv_sem=trecv.at[x],
-            device_id={"ctx": lax.rem(ctx + d * Z, X * Z)}, device_id_type=MESH,
-        )
+        return remote(tbuf.at[x], tbuf.at[x], tsend.at[d - 1], trecv.at[x], on_x(d))
+
+    def state_at(h):
+        return wg.at[me, pl.ds(pl.multiple_of(h * hd, hd), hd)]
 
     def to_member(h, j):
-        return pltpu.make_async_remote_copy(
-            src_ref=wob.at[j], dst_ref=win.at[h], send_sem=osend.at[j], recv_sem=orecv.at[h],
-            device_id={"ctx": base + j}, device_id_type=MESH,
-        )
+        return remote(wob.at[j], state_at(h), osend.at[j], orecv.at[h], {"ctx": base + j})
 
     is_root = (z == root(0)) | (z == root(1))
     mine = lax.rem(z, 4) // 2
@@ -297,10 +401,7 @@
         for j in range(Z):
             @pl.when(z != j)
             def _():
-                pltpu.make_async_remote_copy(
-                    src_ref=mbuf.at[j], dst_ref=mbuf.at[j], send_sem=msend.at[0], recv_sem=mrecv.at[j],
-                    device_id={"ctx": base + lax.rem(z + 1, Z)}, device_id_type=MESH,
-                ).wait_recv()
+                landed(mbuf.at[j], mrecv.at[j])
         ms = [mbuf[j].astype(F32) for j in range(Z)]
         pr = [compose(ms[2 * j + 1], ms[2 * j], hd) for j in range(Z // 2)]
         qd = [compose(pr[2 * j + 1], pr[2 * j], hd) for j in range(Z // 4)]
@@ -310,66 +411,124 @@
             def _():
                 to_group(d).start()
         six = compose(pr[2], qd[0], hd)
-        pre = [None, ms[0], pr[0], compose(ms[2], pr[0], hd), qd[0], compose(ms[4], qd[0], hd), six,
-               compose(ms[6], six, hd)]
+        for j, m in enumerate((ms[0], pr[0], compose(ms[2], pr[0], hd), qd[0], compose(ms[4], qd[0], hd), six,
+                               compose(ms[6], six, hd))):
+            pre[j] = m
+
+    pforward(2)
+    pfar_forward(0)
+
+    @pl.when(is_root)
+    def _():
         wst[...] = w0[mine]
         for j in range(X - 1):
             @pl.when(j < x)
             def _():
-                pltpu.make_async_remote_copy(
-                    src_ref=tbuf.at[j], dst_ref=tbuf.at[j], send_sem=tsend.at[0], recv_sem=trecv.at[j],
-                    device_id={"ctx": lax.rem(ctx + Z, X * Z)}, device_id_type=MESH,
-                ).wait_recv()
+                landed(tbuf.at[j], trecv.at[j])
                 wst[...] = apply_map(tbuf[j].astype(F32), wst[...], hd)
         w = wst[...]
-        for j in range(Z):
-            wob[j] = (w if j == 0 else apply_map(pre[j], w, hd)).astype(BF16)
+        wob[0] = w.astype(BF16)
+        for j in range(1, Z):
+            wob[j] = apply_map(pre[j - 1], w, hd).astype(BF16)
         for j in range(Z):
             @pl.when(z != j)
             def _():
                 to_member(mine, j).start()
-        win[mine] = wob[z]
-
-    gbegin, gshare, gforward, gfar_forward, garrived, gsent = pair_gather(
-        None, ng, width, rows // 2, me, hsend, hrecv)
+        wg[me, pl.ds(pl.multiple_of(mine * hd, hd), hd)] = wob[z]
+
+    pforward(3)
+    for c in range(1, nc):
+        pfar_forward(c)
     for h in hs:
         @pl.when(z != root(h))
         def _():
-            pltpu.make_async_remote_copy(
-                src_ref=win.at[h], dst_ref=win.at[h], send_sem=osend.at[0], recv_sem=orecv.at[h],
-                device_id={"ctx": base + lax.rem(z + 1, Z)}, device_id_type=MESH,
-            ).wait_recv()
-    for c in range(2):
-        rs = slice(c * (rows // 2), (c + 1) * (rows // 2))
-        for h in hs:
-            hc = slice(h * hd, (h + 1) * hd)
-            zv = dot(pbuf[rs, hc], win[h]) + nbuf[rs, hc]
-            zv = zv * lax.rsqrt(jnp.mean(zv * zv, -1, keepdims=True) + 1e-06) * gain[h:h + 1, :]
-            ng[rs, pl.ds(pl.multiple_of(me * width + h * hd, hd), hd)] = zv.astype(BF16)
-        gbegin(c)
-        gshare(c)
-    for c in range(2):
-        gforward(c)
+            landed(state_at(h), orecv.at[h])
+    far = {"tp": lax.rem(me + 4, TP)}
+    sib = me + 1 - 2 * core
+    hop = ({"tp": lax.rem(me + 2, TP)}, {"tp": lax.rem(me + TP - 2, TP)}, far) + ({"tp": sib},) * 4
+    from_me = (0, 0, 0, 0, TP - 2, 2, 4)
+    to_me = (me + TP - 2, me + 2, me + 4, sib, sib + TP - 2, sib + 2, sib + 4)
+
+    def states(j):
+        return wg.at[lax.rem(j, TP)]
+
+    def state_copy(kind):
+        ref = states(me + from_me[kind])
+        return remote(ref, ref, hsend.at[kind], hrecv.at[kind], hop[kind])
+
+    def state_landed(kind):
+        landed(states(to_me[kind]), hrecv.at[kind])
+
+    for kind in range(4):
+        state_copy(kind).start()
+    for k in (0, 2, 4, 5, 6, 7):
+        az_landed(k)
+    for t in range(1, X):
+        landed(b_rows(lax.rem(x + X - t, X)), bxrecv.at[t - 1])
     for t in range(1, TP):
-        from_column(t).wait_recv()
-    wown.wait()
-    for c in range(2):
-        gfar_forward(c)
-    for c in range(2):
-        for kind in (2, 5, 6, 7, 8):
-            garrived(kind, c)
-        rs = slice(c * (rows // 2), (c + 1) * (rows // 2))
-        mixed[rs, :] = jnp.dot(ng[rs, :], wc[...], preferred_element_type=F32).astype(BF16)
+        landed(gall.at[lax.rem(me + TP - t, TP)], yrecv.at[2, t - 1])
+
+    def heads_of(q, first, last):
+        cj = lax.rem(chip + q, Y)
+        blocks_w, parts = [], []
+        for k in range(2):
+            j = 2 * cj + k
+            top = [abuf[:, cx, j].reshape(CH, CH) for cx in range(X)]
+            low = [jnp.concatenate([bbuf[cx, zr * 4 + cz, j] for cx in range(X) for zr in range(2)], 0)
+                   for cz in range(4)]
+            blocks_w += [jnp.concatenate(top, 1), jnp.concatenate(low, 1)]
+            for h in hs:
+                hc = slice(h * hd, (h + 1) * hd)
+                zv = dot(pn[j, :, hc], wg[j, hc, :]) + pn[j, :, width + h * hd:width + (h + 1) * hd].astype(F32)
+                zv = zv * lax.rsqrt(jnp.mean(zv * zv, -1, keepdims=True) + 1e-06)
+                parts.append((zv * gall[j, h:h + 1, :]).astype(BF16))
+        term = jnp.dot(jnp.concatenate(parts, 1), jnp.concatenate(blocks_w, 0), preferred_element_type=F32)
+        if not first:
+            term = total[:, :] + term
+        if last:
+            mixed[:, :] = term.astype(BF16)
+        else:
+            total[:, :] = term
+
+    def gathered(*kinds):
+        for kind in kinds:
+            for c in range(nc):
+                parrived(kind, c)
+
+    gathered(2)
+    state_landed(3)
+    heads_of(0, True, False)
+    for kind in range(3):
+        state_landed(kind)
+        state_copy(kind + 4).start()
+    gathered(5, 6)
+    state_landed(4)
+    heads_of(Y - 1, False, False)
+    state_landed(5)
+    heads_of(1, False, False)
+    gathered(7, 8)
+    state_landed(6)
+    heads_of(2, False, True)
 
     def drain(c, carry):
         sent(c)
+        psent(c)
         return carry
 
     lax.fori_loop(0, nc, drain, 0)
-    for c in range(2):
-        gsent(c)
+    for kind in range(7):
+        state_copy(kind).wait_send()
     for t in range(1, TP):
-        to_column(t).wait_send()
+        y_copy(0, t).wait_send()
+        y_copy(1, t).wait_send()
+        gain_copy(t).wait_send()
+    for t in range(1, X):
+        ax_copy(t).wait_send()
+        bx_copy(t).wait_send()
+    for t in range(1, Z):
+        bz_copy(t).wait_send()
+    for k in range(8):
+        az_copy(k).wait_send()
     for h in hs:
         @pl.when(z != root(h))
         def _():
@@ -410,36 +569,49 @@
             pltpu.SMEM((heads,), F32),
             pltpu.VMEM((heads, hd, hd), F32),
             pltpu.VMEM((heads, hd), F32),
-            pltpu.VMEM((rows, depth), BF16),
-            pltpu.VMEM((depth, 3 * width + CH), BF16),
+            pltpu.VMEM((TP, 8, hd), F32),
+            pltpu.VMEM((TP, rows, feat), BF16),
+            pltpu.VMEM((3, depth, width), BF16),
+            pltpu.VMEM((depth, CH), BF16),
             pltpu.VMEM((CH, depth), F32),
             pltpu.VMEM((rows, 3 * width + CH), F32),
             pltpu.VMEM((heads, hd, 2 * hd), F32),
-            pltpu.VMEM((rows, width), BF16),
-            pltpu.VMEM((rows, width), F32),
             pltpu.VMEM((heads, hd, 2 * hd), BF16),
             pltpu.VMEM((Z, hd, 2 * hd), BF16),
             pltpu.VMEM((X, hd, 2 * hd), BF16),
+            pltpu.VMEM((Z - 1, hd, 2 * hd), F32),
             pltpu.VMEM((hd, hd), F32),
             pltpu.VMEM((Z, hd, hd), BF16),
-            pltpu.VMEM((heads, hd, hd), BF16),
-            pltpu.VMEM((rows, TP * width), BF16),
-            pltpu.VMEM((TP * width, out_cols), BF16),
-            dma((2,)),
+            pltpu.VMEM((TP, rows, 2 * width), BF16),
+            pltpu.VMEM((TP, width, hd), BF16),
+            pltpu.VMEM((Z, X, TP, MB, CH), BF16),
+            pltpu.VMEM((X, Z, TP, MB, CH), BF16),
+            pltpu.VMEM((rows, out_cols), F32),
+            dma((3,)),
             dma((4,)),
             dma((3,)),
             dma((nc, 9)),
             dma((nc, 9)),
-            dma((TP - 1,)),
-            dma((TP - 1,)),
+            dma((nc, 9)),
+            dma((nc, 9)),
+            dma((7,)),
+            dma((7,)),
             dma((heads,)),
             dma((Z,)),
             dma((X - 1,)),
             dma((X,)),
             dma((Z,)),
             dma((heads,)),
-            dma((2, 9)),
-            dma((2, 9)),
+            dma((3, TP - 1)),
+            dma((3, TP - 1)),
+            dma((X - 1,)),
+            dma((X - 1,)),
+            dma((8,)),
+            dma((8,)),
+            dma((Z - 1,)),
+            dma((Z - 1,)),
+            dma((X - 1,)),
+            dma((X - 1,)),
         ],
         compiler_params=pltpu.CompilerParams(
             collective_id=0, has_side_effects=True, vmem_limit_bytes=48 * 1024 * 1024

time: 68.7 us -> 63.1 us (0.918)
  Pallas kernels: 67.8 us -> 62.2 us
    pallas_call x1, Pallas kernels: 67.8 us -> 62.2 us  [local(): pl.pallas_call(layer_kernel, out_shape=jax.ShapeDtypeStruct((rows, out_co...]
where the time goes in v5:
time: 63.1 us; the launch traced here: 63 us
  Pallas kernels  62.2 us (99%)
  local copies, waits for them, and re-layouts  0.8 us (1%)
    pallas_call x1, Pallas kernels, local(): pl.pallas_call(layer_kernel, out_shape=jax.ShapeDtypeStruct((rows, out_co...  62.2 us

profile of v5, /device:TPU:1, one launch (start us, length us, event | category | flops | bytes accessed | tf_op | source)
XLA Modules:
  0.0 63.0 jit_solution(8443513235931031725)
XLA Ops:
  0.0 62.2 %layer.1 = bf16[512,512]{1,0:T(8,128)(2,1)S(1)} custom-call(bf16[512,512]{1,0:T(8,128)(2,1)} %hid.1, bf16[3,4096,256]{2,1,0:T(8,128)(2,1)} %wq.1, bf16[2,4096]{1,0:T(2,128)(2,1)} %bitcast.1, f32[2]{0:T(128)} %lr_in.1, f32[2,128,128]{2,1,0:T(8,128)} %w0_in.1, f32[2,128]{1,0:T(2,128)} %gain_in.1, bf16[256,4096]{1,0:T(8,128)(2,1)} %wout.1), custom_call_target="tpu_custom_call" | custom-call | tf_op jit(solution)/shard_map/layer/pallas_call | solution.py:562
  62.2 0.8 %copy.9 = bf16[512,512]{1,0:T(8,128)(2,1)} copy(bf16[512,512]{1,0:T(8,128)(2,1)S(1)} %layer.1) | data formatting | bytes 1048576

commit v6 on v5

--- a/solution.py
+++ b/solution.py
@@ -236,9 +236,6 @@
     begin(1)
     for c in range(nc):
         share(c)
-    for t in range(1, TP):
-        y_copy(0, t).start()
-        y_copy(1, t).start()
 
     lrt[...] = jnp.zeros_like(lrt)
     for cp in smalls:
@@ -256,29 +253,32 @@
 
     lax.fori_loop(0, wgate.shape[0] // CH, gate, 0)
     pref[...] = jnp.zeros_like(pref)
+    for t in range(1, TP):
+        y_copy(0, t).start()
+        y_copy(1, t).start()
     own.wait()
     for cp in wcopies:
         cp.wait()
 
-    def part(c, q):
-        rs = pl.ds(pl.multiple_of(c * CH, CH), CH)
+    def part(rs, q):
         cj = lax.rem(chip + q, Y)
         ks = pl.ds(pl.multiple_of(cj * 2 * feat, 2 * feat), 2 * feat)
         xs = jnp.concatenate([xg[2 * cj, rs], xg[2 * cj + 1, rs]], 1)
         weights = [wbuf[i, ks, :] for i in range(3)] + [wgate[ks, :]]
         return jnp.concatenate([jnp.dot(xs, w, preferred_element_type=F32) for w in weights], 1)
 
-    def near(c, carry):
-        arrived(2, c)
-        acc[pl.ds(pl.multiple_of(c * CH, CH), CH), :] = part(c, 0)
-        return carry
+    def near():
+        for c in range(nc):
+            arrived(2, c)
+        acc[...] = part(pl.ds(0, rows), 0)
 
     def sides(c):
         arrived(5, c)
         arrived(6, c)
-        acc[pl.ds(pl.multiple_of(c * CH, CH), CH), :] += part(c, 1) + part(c, Y - 1)
-
-    lax.fori_loop(0, nc, near, 0)
+        rs = pl.ds(pl.multiple_of(c * CH, CH), CH)
+        acc[rs, :] += part(rs, 1) + part(rs, Y - 1)
+
+    near()
     forward(0)
     begin(2)
     spread_first()
@@ -297,7 +297,7 @@
         arrived(7, c)
         arrived(8, c)
         rs = pl.ds(pl.multiple_of(c * CH, CH), CH)
-        proj = acc[rs, :] + part(c, 2)
+        proj = acc[rs, :] + part(rs, 2)
         part3 = [[proj[:, (k * heads + h) * hd:(k * heads + h + 1) * hd] for h in hs] for k in range(3)]
 
         def unit(v):
@@ -307,7 +307,11 @@
         k = [unit(part3[1][h]) for h in hs]
         rate = [lr[h] * jax.nn.sigmoid(proj[:, 3 * width + h:3 * width + h + 1]) for h in hs]
         krt = [(k[h] * rate[h]).T.astype(BF16) for h in hs]
-        sg = [dot(jnp.concatenate([q[h], k[h]], 0), krt[h]) for h in hs]
+        qk = [jnp.concatenate([q[h], k[h]], 0).astype(BF16) for h in hs]
+        sg = [dot(qk[h], krt[h]) for h in hs]
+        x0 = [pref[h] for h in hs]
+        qkx = [dot(qk[h], x0[h]) for h in hs]
+        r = [qkx[h][CH:] + jnp.concatenate([k[h], -part3[2][h]], 1) for h in hs]
         m = [jnp.where(causal, sg[h][:CH], 0.0).astype(BF16) for h in hs]
         l1 = [jnp.where(before, sg[h][CH:], 0.0) for h in hs]
         lb = [l1[h].astype(BF16) for h in hs]
@@ -315,18 +319,14 @@
         l34 = [dot(jnp.concatenate([lb[h], l2[h].astype(BF16)], 0), l2[h]) for h in hs]
         t1 = [l2[h] - l1[h] - l34[h][:CH] for h in hs]
         t = [t1[h] + l34[h][CH:] + dot(t1[h], l34[h][CH:]) for h in hs]
-        kv = [jnp.concatenate([k[h], part3[2][h]], 1) for h in hs]
-        uy = [kv[h] + dot(t[h], kv[h]) for h in hs]
-        dn = [dot(jnp.concatenate([krt[h], m[h]], 0), uy[h]) for h in hs]
-        d = [jnp.concatenate([-dn[h][:CH, :hd], dn[h][:CH, hd:]], 1) for h in hs]
-        p = [q[h] - dn[h][CH:, :hd] for h in hs]
-        n = [dn[h][CH:, hd:] for h in hs]
-        x0 = [pref[h] for h in hs]
-        dx = [dot(jnp.concatenate([d[h][:, :hd], p[h]], 0), x0[h]) for h in hs]
+        e = [r[h] + dot(t[h], r[h]) for h in hs]
+        dn = [dot(jnp.concatenate([krt[h], m[h]], 0), e[h]) for h in hs]
         for h in hs:
-            pref[h] = x0[h] + dx[h][:CH] + d[h]
-            pn[me, rs, h * hd:(h + 1) * hd] = (p[h] + dx[h][CH:, :hd]).astype(BF16)
-            pn[me, rs, width + h * hd:width + (h + 1) * hd] = (n[h] + dx[h][CH:, hd:]).astype(BF16)
+            pref[h] = x0[h] - dn[h][:CH]
+            p = q[h] + qkx[h][:CH, :hd] - dn[h][CH:, :hd]
+            n = qkx[h][:CH, hd:] - dn[h][CH:, hd:]
+            pn[me, rs, h * hd:(h + 1) * hd] = p.astype(BF16)
+            pn[me, rs, width + h * hd:width + (h + 1) * hd] = n.astype(BF16)
 
         @pl.when(c < nc - 2)
         def _():
@@ -338,13 +338,18 @@
 
         @pl.when(c == nc - 2)
         def _():
-            for k in range(nc - 1):
+            pbegin(2)
+            pshare(2)
+
+        @pl.when(c < nc - 2)
+        def _():
+            sides(c + 2)
+
+        @pl.when(c == 1)
+        def _():
+            for k in range(2):
                 pbegin(k)
                 pshare(k)
-
-        @pl.when(c < nc - 2)
-        def _():
-            sides(c + 2)
 
         @pl.when(c == 0)
         def _():
@@ -381,7 +386,6 @@
     pbegin(nc - 1)
     pshare(nc - 1)
     pforward(0)
-    az_far()
     pforward(1)
 
     def to_group(d):
@@ -416,7 +420,6 @@
             pre[j] = m
 
     pforward(2)
-    pfar_forward(0)
 
     @pl.when(is_root)
     def _():
@@ -437,7 +440,8 @@
         wg[me, pl.ds(pl.multiple_of(mine * hd, hd), hd)] = wob[z]
 
     pforward(3)
-    for c in range(1, nc):
+    az_far()
+    for c in range(nc):
         pfar_forward(c)
     for h in hs:
         @pl.when(z != root(h))
@@ -572,9 +576,9 @@
             pltpu.VMEM((TP, 8, hd), F32),
             pltpu.VMEM((TP, rows, feat), BF16),
             pltpu.VMEM((3, depth, width), BF16),
-            pltpu.VMEM((depth, CH), BF16),
-            pltpu.VMEM((CH, depth), F32),
-            pltpu.VMEM((rows, 3 * width + CH), F32),
+            pltpu.VMEM((depth, 8), BF16),
+            pltpu.VMEM((8, depth), F32),
+            pltpu.VMEM((rows, 3 * width + 8), F32),
             pltpu.VMEM((heads, hd, 2 * hd), F32),
             pltpu.VMEM((heads, hd, 2 * hd), BF16),
             pltpu.VMEM((Z, hd, 2 * hd), BF16),

time: 63.1 us -> 61.2 us (0.970)
  Pallas kernels: 62.2 us -> 60.2 us
    pallas_call x1, Pallas kernels: 62.2 us -> 60.2 us  [local(): pl.pallas_call(layer_kernel, out_shape=jax.ShapeDtypeStruct((rows, out_co...]
where the time goes in v6:
time: 61.2 us; the launch traced here: 61 us
  Pallas kernels  60.2 us (98%)
  local copies, waits for them, and re-layouts  0.8 us (1%)
    pallas_call x1, Pallas kernels, local(): pl.pallas_call(layer_kernel, out_shape=jax.ShapeDtypeStruct((rows, out_co...  60.2 us

profile of v6, /device:TPU:1, one launch (start us, length us, event | category | flops | bytes accessed | tf_op | source)
XLA Modules:
  0.0 61.0 jit_solution(15341030352581622953)
XLA Ops:
  0.0 60.2 %layer.1 = bf16[512,512]{1,0:T(8,128)(2,1)S(1)} custom-call(bf16[512,512]{1,0:T(8,128)(2,1)} %hid.1, bf16[3,4096,256]{2,1,0:T(8,128)(2,1)} %wq.1, bf16[2,4096]{1,0:T(2,128)(2,1)} %bitcast.1, f32[2]{0:T(128)} %lr_in.1, f32[2,128,128]{2,1,0:T(8,128)} %w0_in.1, f32[2,128]{1,0:T(2,128)} %gain_in.1, bf16[256,4096]{1,0:T(8,128)(2,1)} %wout.1), custom_call_target="tpu_custom_call" | custom-call | tf_op jit(solution)/shard_map/layer/pallas_call | solution.py:566
  60.2 0.8 %copy.9 = bf16[512,512]{1,0:T(8,128)(2,1)} copy(bf16[512,512]{1,0:T(8,128)(2,1)S(1)} %layer.1) | data formatting | bytes 1048576

commit v7 on v6

--- a/solution.py
+++ b/solution.py
@@ -89,7 +89,7 @@
 
 
 def layer_kernel(hid, wq, lrw_in, lr_in, w0_in, gain_in, wout, mixed,
-                 lrw, lr, w0, gain, gall, xg, wbuf, wgate, lrt, acc, pref, xbf, mbuf, tbuf, pre, wst, wob, pn, wg, abuf, bbuf, total,
+                 lrw, lr, w0, gain, gall, xg, wbuf, wgate, lrt, acc, pref, xbf, mbuf, tbuf, pre, prb, wst, wob, pn, wg, abuf, bbuf, total,
                  loc, lsem, wsem, gsend, grecv, psend, precv, hsend, hrecv, msend, mrecv, tsend, trecv, osend, orecv,
                  ysend, yrecv, axsend, axrecv, azsend, azrecv, bzsend, bzrecv, bxsend, bxrecv):
     rows, feat = hid.shape
@@ -418,6 +418,7 @@
         for j, m in enumerate((ms[0], pr[0], compose(ms[2], pr[0], hd), qd[0], compose(ms[4], qd[0], hd), six,
                                compose(ms[6], six, hd))):
             pre[j] = m
+            prb[j * hd:(j + 1) * hd, :] = m[:, :hd].astype(BF16)
 
     pforward(2)
 
@@ -430,9 +431,10 @@
                 landed(tbuf.at[j], trecv.at[j])
                 wst[...] = apply_map(tbuf[j].astype(F32), wst[...], hd)
         w = wst[...]
+        prod = jnp.dot(prb[...], w.astype(BF16), preferred_element_type=F32)
         wob[0] = w.astype(BF16)
         for j in range(1, Z):
-            wob[j] = apply_map(pre[j - 1], w, hd).astype(BF16)
+            wob[j] = (w + prod[(j - 1) * hd:j * hd] + pre[j - 1][:, hd:]).astype(BF16)
         for j in range(Z):
             @pl.when(z != j)
             def _():
@@ -443,28 +445,28 @@
     az_far()
     for c in range(nc):
         pfar_forward(c)
-    for h in hs:
-        @pl.when(z != root(h))
-        def _():
-            landed(state_at(h), orecv.at[h])
     far = {"tp": lax.rem(me + 4, TP)}
     sib = me + 1 - 2 * core
     hop = ({"tp": lax.rem(me + 2, TP)}, {"tp": lax.rem(me + TP - 2, TP)}, far) + ({"tp": sib},) * 4
     from_me = (0, 0, 0, 0, TP - 2, 2, 4)
     to_me = (me + TP - 2, me + 2, me + 4, sib, sib + TP - 2, sib + 2, sib + 4)
 
-    def states(j):
-        return wg.at[lax.rem(j, TP)]
-
-    def state_copy(kind):
-        ref = states(me + from_me[kind])
-        return remote(ref, ref, hsend.at[kind], hrecv.at[kind], hop[kind])
-
-    def state_landed(kind):
-        landed(states(to_me[kind]), hrecv.at[kind])
-
-    for kind in range(4):
-        state_copy(kind).start()
+    def states(j, h):
+        return wg.at[lax.rem(j, TP), pl.ds(h * hd, hd)]
+
+    def state_copy(kind, h):
+        ref = states(me + from_me[kind], h)
+        return remote(ref, ref, hsend.at[kind, h], hrecv.at[kind, h], hop[kind])
+
+    def state_landed(kind, h):
+        landed(states(to_me[kind], h), hrecv.at[kind, h])
+
+    for h in hs:
+        @pl.when(z != root(h))
+        def _():
+            landed(state_at(h), orecv.at[h])
+        for kind in (2, 0, 1, 3):
+            state_copy(kind, h).start()
     for k in (0, 2, 4, 5, 6, 7):
         az_landed(k)
     for t in range(1, X):
@@ -500,18 +502,23 @@
                 parrived(kind, c)
 
     gathered(2)
-    state_landed(3)
+    for h in hs:
+        state_landed(3, h)
     heads_of(0, True, False)
     for kind in range(3):
-        state_landed(kind)
-        state_copy(kind + 4).start()
+        for h in hs:
+            state_landed(kind, h)
+            state_copy(kind + 4, h).start()
     gathered(5, 6)
-    state_landed(4)
+    for h in hs:
+        state_landed(4, h)
     heads_of(Y - 1, False, False)
-    state_landed(5)
+    for h in hs:
+        state_landed(5, h)
     heads_of(1, False, False)
     gathered(7, 8)
-    state_landed(6)
+    for h in hs:
+        state_landed(6, h)
     heads_of(2, False, True)
 
     def drain(c, carry):
@@ -521,7 +528,8 @@
 
     lax.fori_loop(0, nc, drain, 0)
     for kind in range(7):
-        state_copy(kind).wait_send()
+        for h in hs:
+            state_copy(kind, h).wait_send()
     for t in range(1, TP):
         y_copy(0, t).wait_send()
         y_copy(1, t).wait_send()
@@ -584,6 +592,7 @@
             pltpu.VMEM((Z, hd, 2 * hd), BF16),
             pltpu.VMEM((X, hd, 2 * hd), BF16),
             pltpu.VMEM((Z - 1, hd, 2 * hd), F32),
+            pltpu.VMEM(((Z - 1) * hd, hd), BF16),
             pltpu.VMEM((hd, hd), F32),
             pltpu.VMEM((Z, hd, hd), BF16),
             pltpu.VMEM((TP, rows, 2 * width), BF16),
@@ -598,8 +607,8 @@
             dma((nc, 9)),
             dma((nc, 9)),
             dma((nc, 9)),
-            dma((7,)),
-            dma((7,)),
+            dma((7, heads)),
+            dma((7, heads)),
             dma((heads,)),
             dma((Z,)),
             dma((X - 1,)),

time: 61.2 us -> 60.9 us (level)
  no operation moved by 1% of the time
where the time goes in v7:
time: 60.9 us; the launch traced here: 60.8 us
  Pallas kernels  60 us (99%)
  local copies, waits for them, and re-layouts  0.8 us (1%)
    pallas_call x1, Pallas kernels, local(): pl.pallas_call(layer_kernel, out_shape=jax.ShapeDtypeStruct((rows, out_co...  60 us

profile of v7, /device:TPU:1, one launch (start us, length us, event | category | flops | bytes accessed | tf_op | source)
XLA Modules:
  0.0 60.8 jit_solution(16569612466699903874)
XLA Ops:
  0.0 60.0 %layer.1 = bf16[512,512]{1,0:T(8,128)(2,1)S(1)} custom-call(bf16[512,512]{1,0:T(8,128)(2,1)} %hid.1, bf16[3,4096,256]{2,1,0:T(8,128)(2,1)} %wq.1, bf16[2,4096]{1,0:T(2,128)(2,1)} %bitcast.1, f32[2]{0:T(128)} %lr_in.1, f32[2,128,128]{2,1,0:T(8,128)} %w0_in.1, f32[2,128]{1,0:T(2,128)} %gain_in.1, bf16[256,4096]{1,0:T(8,128)(2,1)} %wout.1), custom_call_target="tpu_custom_call" | custom-call | tf_op jit(solution)/shard_map/layer/pallas_call | solution.py:574
  60.0 0.8 %copy.9 = bf16[512,512]{1,0:T(8,128)(2,1)} copy(bf16[512,512]{1,0:T(8,128)(2,1)S(1)} %layer.1) | data formatting | bytes 1048576

commit v8 on v7

--- a/solution.py
+++ b/solution.py
@@ -410,6 +410,10 @@
         pr = [compose(ms[2 * j + 1], ms[2 * j], hd) for j in range(Z // 2)]
         qd = [compose(pr[2 * j + 1], pr[2 * j], hd) for j in range(Z // 4)]
         tbuf[x] = compose(qd[1], qd[0], hd).astype(BF16)
+        @pl.when(x == 0)
+        def _():
+            tbuf[0, :, :hd] = apply_map(tbuf[0].astype(F32), w0[mine], hd).astype(BF16)
+
         for d in range(1, X):
             @pl.when(x + d < X)
             def _():
@@ -429,7 +433,8 @@
             @pl.when(j < x)
             def _():
                 landed(tbuf.at[j], trecv.at[j])
-                wst[...] = apply_map(tbuf[j].astype(F32), wst[...], hd)
+                m = tbuf[j].astype(F32)
+                wst[...] = m[:, :hd] if j == 0 else apply_map(m, wst[...], hd)
         w = wst[...]
         prod = jnp.dot(prb[...], w.astype(BF16), preferred_element_type=F32)
         wob[0] = w.astype(BF16)

time: 60.9 us -> 60.9 us (level)
  no operation moved by 1% of the time
where the time goes in v8:
time: 60.9 us; the launch traced here: 60.8 us
  Pallas kernels  60 us (99%)
  local copies, waits for them, and re-layouts  0.8 us (1%)
    pallas_call x1, Pallas kernels, local(): pl.pallas_call(layer_kernel, out_shape=jax.ShapeDtypeStruct((rows, out_co...  60 us

profile of v8, /device:TPU:1, one launch (start us, length us, event | category | flops | bytes accessed | tf_op | source)
XLA Modules:
  0.0 60.8 jit_solution(128192208555665890)
XLA Ops:
  0.0 60.0 %layer.1 = bf16[512,512]{1,0:T(8,128)(2,1)S(1)} custom-call(bf16[512,512]{1,0:T(8,128)(2,1)} %hid.1, bf16[3,4096,256]{2,1,0:T(8,128)(2,1)} %wq.1, bf16[2,4096]{1,0:T(2,128)(2,1)} %bitcast.1, f32[2]{0:T(128)} %lr_in.1, f32[2,128,128]{2,1,0:T(8,128)} %w0_in.1, f32[2,128]{1,0:T(2,128)} %gain_in.1, bf16[256,4096]{1,0:T(8,128)(2,1)} %wout.1), custom_call_target="tpu_custom_call" | custom-call | tf_op jit(solution)/shard_map/layer/pallas_call | solution.py:579
  60.0 0.8 %copy.9 = bf16[512,512]{1,0:T(8,128)(2,1)} copy(bf16[512,512]{1,0:T(8,128)(2,1)S(1)} %layer.1) | data formatting | bytes 1048576
